TPU v7x, 128 devices: a whole 4x4x4 slice. The times are simulated.
128 devices in a mesh: site: 16 (over x, y), scen: 8 (over z, core).
Axes of the slice: x: 4, y: 4, z: 4, core: 2. Of those that a mesh axis runs over, the one named last changes fastest.
Arguments:
- normals: bfloat16 [40960, 2688], P('site', 'scen'), may hold values from -6 to 6
- pattern: int32 [64, 40], replicated, may hold values from 0 to 159, as said below
- factor: bfloat16 [64, 40, 256, 256], P('site', None, 'scen'), may hold values from -0.0625 to 0.0625
- temporal: bfloat16 [168, 168], replicated, may hold values from -0.5 to 0.5
- capacity: float32 [16384], P('site'), may hold values from 0.05 to 0.4
- spread: float32 [16384], P('site'), may hold values from 0.2 to 0.8
- bus_map: int32 [16384], replicated, may hold values from 0 to 1023
Outputs:
- bus_power: float32 [1024, 2688], P('site', 'scen')
Inputs may be any that keep to these rules, and one draw needn't show every extreme that they name: `pattern`: each block row names 40 different column blocks. The 4 block rows of one index of site (rows k * 4 to (k + 1) * 4 - 1) name at most 5 different column blocks among those held by any one index of site (blocks j * 10 to (j + 1) * 10 - 1), and exactly 5 among those held by index k itself.
All inputs are finite; a program needn't handle non-finite values.
Results may differ from a plain program's by a relative error of at most 0.0013.
Values may be sent and summed in bfloat16 or wider, within the bound.
No kernel may reach another device: no remote copies, remote signals or barrier semaphores. Data moves between devices by JAX's collectives and lax.ppermute only.
A program may use at most 192 MiB of HBM per device.

v0:
```python
import jax
import jax.numpy as jnp
from jax import lax
from jax.sharding import PartitionSpec as P

BLK = 256
HOURS = 168
NZ = 40
MAX_COLUMN_BLOCKS = 5
RB_DEV = 4
BUS_DEV = 64


def in_blocks(value, dim, devices):
    dims = value.shape
    tiles = value.reshape(*dims[:dim], devices, dims[dim] // devices, *dims[dim + 1 :])
    return jnp.moveaxis(tiles, dim, 0)


def cut_rows(length, count):
    turn = length // count
    if turn >= 8:
        turn -= turn % 8
    return [turn * k for k in range(1, count)]


def laid_out(tiles, dim):
    tiles = jnp.moveaxis(tiles, 0, dim)
    dims = tiles.shape
    return tiles.reshape(*dims[:dim], dims[dim] * dims[dim + 1], *dims[dim + 2 :])


def exchange_in_pieces(value, axis, pieces, split_dim, concat_dim):
    tiles = in_blocks(value, split_dim, lax.axis_size(axis))
    cut = max(range(1, max(2, tiles.ndim - 1)), key=lambda d: tiles.shape[d])
    outs = []
    for piece in jnp.split(tiles, cut_rows(tiles.shape[cut], pieces), axis=cut):
        if piece.size:
            outs.append(lax.all_to_all(piece, axis, split_axis=0, concat_axis=0, tiled=True))
    return laid_out(jnp.concatenate(outs, axis=cut), concat_dim)


def summed_on_arrival(value, axis, dim):
    devices = lax.axis_size(axis)
    tiles = lax.all_to_all(in_blocks(value, dim, devices), axis, 0, 0, tiled=True)
    return jnp.sum(tiles, axis=0)


def shards(normals, pattern, factor, temporal, capacity, spread, bus_map):
    own_index = lax.axis_index("site")
    site_count = lax.axis_size("site")
    row_width = normals.shape[1]
    scen_here = row_width // HOURS
    local_blocks = normals.reshape(-1, BLK, row_width)
    block_count = local_blocks.shape[0]
    all_blocks = block_count * site_count
    my_columns = lax.dynamic_slice_in_dim(pattern, own_index * RB_DEV, RB_DEV, 0).reshape(-1)
    block_ids = jnp.arange(all_blocks, dtype=jnp.int32)
    wanted = pattern.reshape(site_count, -1)
    needed = jnp.any(wanted[:, :, None] == block_ids[None, None, :], axis=1)
    owned_need = lax.dynamic_slice_in_dim(needed, own_index * block_count, block_count, 1).astype(
        jnp.int32
    )
    slot_rank = jnp.cumsum(owned_need, axis=1) - 1
    slot_ids = jnp.arange(MAX_COLUMN_BLOCKS, dtype=jnp.int32)
    chosen = (owned_need[:, None, :] == 1) & (slot_rank[:, None, :] == slot_ids[None, :, None])
    local_ids = jnp.arange(block_count, dtype=jnp.int32)
    block_index = jnp.sum(jnp.where(chosen, local_ids[None, None, :], 0), axis=2)
    present = jnp.any(chosen, axis=2)
    outgoing = jnp.where(
        present[:, :, None, None], local_blocks[block_index], jnp.zeros((), normals.dtype)
    )
    arrived = exchange_in_pieces(outgoing, "site", 2, 0, 0)
    my_need = lax.dynamic_index_in_dim(needed, own_index, 0, keepdims=False).astype(jnp.int32)
    my_rank = (jnp.cumsum(my_need.reshape(site_count, block_count), axis=1) - 1).reshape(-1)
    slot_of = my_columns // block_count * MAX_COLUMN_BLOCKS + my_rank[my_columns]
    picked = jnp.take(
        arrived.reshape(site_count * MAX_COLUMN_BLOCKS, BLK, row_width), slot_of, axis=0
    )
    picked = picked.reshape(RB_DEV, NZ, BLK, row_width)
    capacity_rows = capacity.reshape(RB_DEV, BLK)
    spread_rows = spread.reshape(RB_DEV, BLK)
    portion = lax.all_gather(factor, "scen", axis=2, tiled=True)
    height = portion.shape[2]
    spatial = jnp.einsum(
        "ktij,ktjw->kiw", portion, picked, preferred_element_type=jnp.float32
    ).astype(jnp.bfloat16)
    hourly = spatial.reshape(RB_DEV, height, scen_here, HOURS)
    weather = jnp.einsum("kpsg,hg->kpsh", hourly, temporal, preferred_element_type=jnp.float32)
    scale_part = capacity_rows[:, :, None, None]
    spread_part = spread_rows[:, :, None, None]
    values = scale_part * jnp.exp(spread_part * weather - 0.5 * spread_part * spread_part)
    injected = (
        values.astype(jnp.bfloat16)
        .reshape(RB_DEV, height, row_width)
        .reshape(RB_DEV * BLK, row_width)
    )
    site_total = RB_DEV * BLK
    my_buses = lax.dynamic_slice_in_dim(bus_map, own_index * site_total, site_total, 0)
    wanted_buses = jnp.arange(BUS_DEV * lax.axis_size("site"), dtype=jnp.int32)
    onehot_rows = (my_buses[None, :] == wanted_buses[:, None]).astype(jnp.bfloat16)
    return summed_on_arrival(
        jnp.dot(onehot_rows, injected, preferred_element_type=jnp.float32), "site", 0
    )


def solution(mesh):
    placed = (P("site", "scen"), P(), P("site", None, "scen", None), P(), P("site"), P("site"), P())
    return jax.shard_map(
        shards, mesh=mesh, in_specs=placed, out_specs=P("site", "scen"), check_vma=False
    )
```

profile of v0, /device:TPU:64, one launch (start us, length us, event | category | flops | bytes accessed | tf_op | source)
XLA Modules:
  0.0 324.0 jit_solution(16282770276139524524)
XLA Ops:
  6.5 0.0 copy-start
  6.5 0.0 all-gather.2.cloned.1.call-start
  6.5 0.7 all-gather.2.cloned.1.call-update
  7.3 0.8 copy.16
  8.1 0.1 eq.65
  8.1 0.5 fusion.6
  8.7 0.1 broadcast_compare_fusion
  8.7 0.2 reduce_window_sum.18
  8.9 0.2 select_reduce_fusion
  9.1 0.1 copy.20
  9.2 0.1 reshape.200
  9.3 3.9 %copy.19 = bf16[2560,336]{1,0:T(8,128)(2,1)} copy(bf16[2560,336]{0,1:T(8,128)(2,1)} %param.7) | data formatting | bytes 3440640 | tf_op args[0]
  13.2 2.8 copy.21
  16.0 0.2 fusion.21
  16.2 0.1 copy.18
  16.3 9.2 %gather_fusion.1 = bf16[80,256,336]{1,2,0:T(8,128)(2,1)} fusion(bf16[10,256,336]{1,2,0:T(8,128)(2,1)S(1)} %copy.21, s32[1024]{0:T(1024)S(1)} %pad_clamp_fusion.1), kind=kCustom, calls=%fused_computation.1 | custom fusion | bytes 27525440 | tf_op jit(solution)/shard_map/gather | solution.py:71
  25.5 7.7 %broadcast_select_fusion = bf16[16,1,5,256,336]{3,4,2,1,0:T(8,128)(2,1)S(1)} fusion(bf16[16,1,5,256,336]{3,4,2,1,0:T(8,128)(2,1)} %bitcast.30, pred[16,5]{1,0:T(8,128)(4,1)S(1)} %copy.18), kind=kLoop, calls=%fused_computation.8 | loop fusion | flops 6881280 | bytes 27525200 | tf_op jit(solution)/shard_map/jit(_where)/select_n | solution.py:70
  33.2 4.6 %fusion.25 = (bf16[16,1,5,128,336]{3,4,2,1,0:T(8,128)(2,1)S(1)}, bf16[16,1,5,128,336]{3,4,2,1,0:T(8,128)(2,1)}) fusion(bf16[16,1,5,256,336]{3,4,2,1,0:T(8,128)(2,1)S(1)} %broadcast_select_fusion), kind=kLoop, calls=%fused_computation.50 | loop fusion | bytes 27525120 | tf_op jit(solution)/shard_map/split | solution.py:37
  37.8 0.0 copy-start.1
  37.8 0.0 copy-start.2
  37.8 87.9 %all_to_all.15 = bf16[16,1,5,128,336]{3,4,2,1,0:T(8,128)(2,1)} all-to-all(bf16[16,1,5,128,336]{3,4,2,1,0:T(8,128)(2,1)S(1)} %get-tuple-element.5), channel_id=1, replica_groups=mesh['site'=16,'scen'=8] {'site'}, dimensions={0} | all-to-all | bytes 13762560 | tf_op jit(solution)/shard_map/all_to_all | solution.py:39
  125.7 4.7 %all-to-all-start.1 = ((bf16[16,1,5,128,336]{3,4,2,1,0:T(8,128)(2,1)}), bf16[16,1,5,128,336]{3,4,2,1,0:T(8,128)(2,1)}, u32[]{:S(2)}, u32[]{:S(2)}) async-start(bf16[16,1,5,128,336]{3,4,2,1,0:T(8,128)(2,1)} %get-tuple-element.6), calls=%async_computation.1 | async-start | bytes 13762560 | tf_op jit(solution)/shard_map/all_to_all | solution.py:39
  130.4 0.1 reshape.186
  130.5 0.1 reshape.189
  130.6 0.2 reduce_window_sum.17
  130.7 0.1 sub.26
  130.8 1.6 gather_fusion
  132.5 0.1 gather.19
  132.6 0.0 copy-done.1
  132.6 0.0 copy-done.2
  132.7 105.7 %all-to-all-done.1 = bf16[16,1,5,128,336]{3,4,2,1,0:T(8,128)(2,1)} async-done(((bf16[16,1,5,128,336]{3,4,2,1,0:T(8,128)(2,1)}), bf16[16,1,5,128,336]{3,4,2,1,0:T(8,128)(2,1)}, u32[]{:S(2)}, u32[]{:S(2)}) %all-to-all-start.1) | async-done | bytes 6881312 | tf_op jit(solution)/shard_map/all_to_all | solution.py:39
  238.4 12.8 %pad_maximum_fusion = bf16[16,1,5,256,336]{3,4,2,1,0:T(8,128)(2,1)} fusion(bf16[16,1,5,128,336]{3,4,2,1,0:T(8,128)(2,1)} %all-to-all-done.1, bf16[16,1,5,128,336]{3,4,2,1,0:T(8,128)(2,1)} %all_to_all.15), kind=kLoop, calls=%fused_computation.6 | loop fusion | flops 27525120 | bytes 27525120 | tf_op jit(solution)/shard_map/concatenate | solution.py:40
  251.2 16.8 %gather_fusion.2 = bf16[160,256,336]{1,2,0:T(8,128)(2,1)} fusion(bf16[80,256,336]{1,2,0:T(8,128)(2,1)} %bitcast.29, s32[1024]{0:T(1024)S(1)} %pad_clamp_fusion), kind=kCustom, calls=%fused_computation.2 | custom fusion | bytes 55050880 | tf_op jit(solution)/shard_map/jit(_take)/gather | solution.py:77
  268.0 0.0 all-gather.2.cloned.1.call-done
  268.0 0.0 dynamic-slice-start
  268.1 17.8 %fusion.16 = bf16[4,336,256]{2,1,0:T(8,128)(2,1)S(1)} fusion(bf16[4,40,256,256]{3,2,1,0:T(8,128)(2,1)} %all-gather.2.cloned.1.call-done, bf16[4,40,256,336]{2,3,1,0:T(8,128)(2,1)} %bitcast.31, pred[4,40]{1,0:T(4,128)(4,1)S(1)} %compare_and_fusion), kind=kOutput, calls=%fused_computation.21 | convolution fusion | flops 7060537344 | bytes 49184928 | tf_op jit(solution)/shard_map/ktij,ktjw->kiw/dot_general | solution.py:85
  285.9 0.0 copy-done
  285.9 0.4 fusion.15
  286.3 0.4 copy.22
  286.7 0.5 reshape.218
  287.2 0.0 dynamic-slice-done
  287.2 1.3 fusion.4
  288.5 27.9 %all_to_all.16 = f32[16,64,336]{2,1,0:T(8,128)S(1)} all-to-all(f32[16,64,336]{2,1,0:T(8,128)S(1)} %fusion.4), channel_id=1, replica_groups=mesh['site'=16,'scen'=8] {'site'}, dimensions={0} | all-to-all | bytes 2752512 | tf_op jit(solution)/shard_map/all_to_all | solution.py:45
  316.4 0.7 reduce_sum.22
  (15 shorter events, 0.1 us)
Async XLA Ops:
  6.5 279.3 %copy-start = (bf16[168,168]{1,0:T(8,128)(2,1)S(1)}, bf16[168,168]{1,0:T(8,128)(2,1)}, u32[]{:S(2)}) copy-start(bf16[168,168]{1,0:T(8,128)(2,1)} %param.10) | copy-start | bytes 169348
  6.5 261.5 %all-gather.2.cloned.1.call-start = ((), (), s32[]{:S(2)}) async-start(), calls=%async_computation.3 | async-start | bytes 23592960 | tf_op jit(solution)/shard_map/all_gather | solution.py:83
  37.8 94.7 %copy-start.1 = (f32[1024]{0:T(1024)S(1)}, f32[1024]{0:T(1024)}, u32[]{:S(2)}) copy-start(f32[1024]{0:T(1024)} %param.12) | copy-start | bytes 12292
  37.8 94.7 %copy-start.2 = (f32[1024]{0:T(1024)S(1)}, f32[1024]{0:T(1024)}, u32[]{:S(2)}) copy-start(f32[1024]{0:T(1024)} %param.11) | copy-start | bytes 12292
  125.7 112.7 %all-to-all-start.1 = ((bf16[16,1,5,128,336]{3,4,2,1,0:T(8,128)(2,1)}), bf16[16,1,5,128,336]{3,4,2,1,0:T(8,128)(2,1)}, u32[]{:S(2)}, u32[]{:S(2)}) async-start(bf16[16,1,5,128,336]{3,4,2,1,0:T(8,128)(2,1)} %get-tuple-element.6), calls=%async_computation.1 | async-start | bytes 13762560 | tf_op jit(solution)/shard_map/all_to_all | solution.py:39
  268.0 19.1 %dynamic-slice-start = ((s32[16384]{0:T(1024)}, s32[]{:T(128)}), s32[1024]{0:T(1024)S(1)}, s32[]{:S(2)}) async-start(s32[16384]{0:T(1024)} %param.13, s32[]{:T(128)} %select_n.86), calls=%async_computation.4 | async-start | bytes 8704 | tf_op jit(solution)/shard_map/dynamic_slice | solution.py:99
Sparse Core Ops, SparseCore 0:
  9.1 103.8 all-gather.1
where the time goes:
time: 325 us; the launch traced here: 324 us
  blocking collectives  116 us (36%)
  waiting for transfers between devices  106 us (33%)
  local copies, waits for them, and re-layouts  41.3 us (13%)
  other arithmetic  22.7 us (7%)
  matrix products  19.5 us (6%)
  between operations  13.6 us (4%)
  starting transfers between devices  4.66 us (1%)
    all_to_all x1, waiting for transfers between devices, exchange_in_pieces(): lax.all_to_all(piece, axis, split_axis=0, concat_axis=0, tiled=True)  106 us
    all_to_all x1, blocking collectives, exchange_in_pieces(): lax.all_to_all(piece, axis, split_axis=0, concat_axis=0, tiled=True)  87.9 us
    all_to_all x1, blocking collectives, summed_on_arrival(): lax.all_to_all(in_blocks(value, dim, devices), axis, 0, 0, tiled=True)  27.9 us
    dot_general x1, matrix products, shards(): jnp.einsum('ktij,ktjw->kiw', portion, picked, preferred_element_type=jnp....  17.8 us
    gather x1, local copies, waits for them, and re-layouts, shards(): jnp.take(arrived.reshape(site_count * MAX_COLUMN_BLOCKS, BLK, row_width),...  16.8 us
    concatenate x1, other arithmetic, exchange_in_pieces(): return laid_out(jnp.concatenate(outs, axis=cut), concat_dim)  12.8 us
    gather x1, local copies, waits for them, and re-layouts, shards(): local_blocks[block_index]  9.21 us
    select_n x1, other arithmetic, shards(): jnp.where(present[:, :, None, None], local_blocks[block_index], jnp.zeros...  7.73 us
  transfers between devices with their start and end apart: 2, of which 1 were waited for; matrix products, arithmetic and copies ran while one was open for 19% of the time, Pallas kernels for 0%

commit v1 on v0

v1 whole, which is shorter than its diff:
```python
import functools

import jax
import jax.numpy as jnp
from jax import lax
from jax.experimental import pallas as pl
from jax.experimental.pallas import tpu as pltpu
from jax.sharding import PartitionSpec as P

BLK = 256
HALF = 128
HOURS = 168
NZ = 40
SLOTS = 5
RB_DEV = 4
CB_DEV = 10
SIDE = 4
CHUNK = 10
BUSES = 1024


def shift(value, dx, dy):
    n = SIDE
    pairs = [
        (x * n + y, ((x + dx) % n) * n + (y + dy) % n) for x in range(n) for y in range(n)
    ]
    return lax.ppermute(value, "site", pairs)


def step(value, axis, d):
    return shift(value, d, 0) if axis == 0 else shift(value, 0, d)


def transpose_kernel(z_ref, lo_ref, hi_ref):
    z = z_ref[...].T
    lo_ref[0] = z[:, :HALF]
    hi_ref[0] = z[:, HALF:]


def transposed(normals):
    blocks = normals.shape[0] // BLK
    width = normals.shape[1]
    out = jax.ShapeDtypeStruct((blocks, width, HALF), normals.dtype)
    spec = pl.BlockSpec((1, width, HALF), lambda b: (b, 0, 0))
    return pl.pallas_call(
        transpose_kernel,
        grid=(blocks,),
        in_specs=[pl.BlockSpec((BLK, width), lambda b: (b, 0))],
        out_specs=[spec, spec],
        out_shape=[out, out],
    )(normals)


def slots_of(ex, ey):
    return (ex * SIDE + ey) * SLOTS


def main_kernel(
    slot_ref, own_ref, *refs
):
    (lo_line, hi_line, lo_p, lo_q, hi_p, hi_q) = (
        refs[0:4], refs[4:8], refs[8:11], refs[11:14], refs[14:17], refs[17:20]
    )
    f_ref, temporal_ref, cap_ref, spr_ref, bus_ref, out_ref, zlo, zhi, acc, power, sem = refs[20:]
    r, c = pl.program_id(0), pl.program_id(1)

    def copies(fn):
        for ex in range(SIDE):
            for ey in range(SIDE):
                base = slots_of(ex, ey)
                for s in range(SLOTS):
                    local = own_ref[base + s]
                    if ey == 0:
                        src = lo_line[ex].at[local]
                    elif ex == 0:
                        src = lo_p[SIDE - 1 - ey].at[s]
                    else:
                        src = lo_q[SIDE - 1 - ey].at[(ex - 1) * SLOTS + s]
                    fn(pltpu.make_async_copy(src, zlo.at[base + s], sem))
                    if ex == 0:
                        src = hi_line[ey].at[local]
                    elif ey == 0:
                        src = hi_p[SIDE - 1 - ex].at[s]
                    else:
                        src = hi_q[SIDE - 1 - ex].at[(ey - 1) * SLOTS + s]
                    fn(pltpu.make_async_copy(src, zhi.at[base + s], sem))

    @pl.when((r == 0) & (c == 0))
    def _():
        copies(lambda d: d.start())
        power[...] = jnp.zeros_like(power)
        copies(lambda d: d.wait())

    @pl.when(c == 0)
    def _():
        acc[...] = jnp.zeros_like(acc)

    total = acc[...]
    for tt in range(CHUNK):
        slot = slot_ref[r * NZ + c * CHUNK + tt]
        z = jnp.concatenate([zlo[slot], zhi[slot]], axis=1)
        total += lax.dot_general(
            z, f_ref[0, tt], (((1,), (1,)), ((), ())), preferred_element_type=jnp.float32
        )
    acc[...] = total

    @pl.when(c == pl.num_programs(1) - 1)
    def _():
        cap, spr = cap_ref[0], spr_ref[0]
        parts = []
        for s in range(acc.shape[0] // HOURS):
            sp = acc[s * HOURS : (s + 1) * HOURS, :].astype(jnp.bfloat16)
            w = jnp.dot(temporal_ref[...], sp, preferred_element_type=jnp.float32)
            parts.append(cap * jnp.exp(spr * w - 0.5 * spr * spr))
        inj = jnp.concatenate(parts, axis=0).astype(jnp.bfloat16)
        buses = lax.broadcasted_iota(jnp.int32, (BUSES, BLK), 0)
        onehot = jnp.where(buses == bus_ref[0], 1.0, 0.0).astype(jnp.bfloat16)
        power[...] += lax.dot_general(
            onehot, inj, (((1,), (1,)), ((), ())), preferred_element_type=jnp.float32
        )

    @pl.when((c == pl.num_programs(1) - 1) & (r == pl.num_programs(0) - 1))
    def _():
        out_ref[...] = power[...].astype(jnp.bfloat16)


def main(slots, own, arrays, factor, temporal, cap, spr, bus, width):
    any_spec = pl.BlockSpec(memory_space=pl.ANY)
    vec = pl.BlockSpec((1, 1, BLK), lambda r, c, *_: (r, 0, 0))
    grid_spec = pltpu.PrefetchScalarGridSpec(
        num_scalar_prefetch=2,
        grid=(RB_DEV, NZ // CHUNK),
        in_specs=[any_spec] * len(arrays)
        + [
            pl.BlockSpec((1, CHUNK, BLK, BLK), lambda r, c, *_: (r, c, 0, 0)),
            pl.BlockSpec((HOURS, HOURS), lambda r, c, *_: (0, 0)),
            vec,
            vec,
            vec,
        ],
        out_specs=pl.BlockSpec((BUSES, width), lambda r, c, *_: (0, 0)),
        scratch_shapes=[
            pltpu.VMEM((SIDE * SIDE * SLOTS, width, HALF), jnp.bfloat16),
            pltpu.VMEM((SIDE * SIDE * SLOTS, width, HALF), jnp.bfloat16),
            pltpu.VMEM((width, BLK), jnp.float32),
            pltpu.VMEM((BUSES, width), jnp.float32),
            pltpu.SemaphoreType.DMA,
        ],
    )
    return pl.pallas_call(
        main_kernel,
        grid_spec=grid_spec,
        out_shape=jax.ShapeDtypeStruct((BUSES, width), jnp.bfloat16),
        compiler_params=pltpu.CompilerParams(vmem_limit_bytes=48 << 20),
    )(slots, own, *arrays, factor, temporal, cap, spr, bus)


def shards(normals, pattern, factor, temporal, capacity, spread, bus_map):
    width = normals.shape[1]
    n = SIDE
    sites = n * n
    me = lax.axis_index("site")
    x, y = me // n, me % n
    portion = lax.all_gather(factor, "scen", axis=2, tiled=True)

    ids = jnp.arange(sites * CB_DEV, dtype=jnp.int32)
    wanted = pattern.reshape(sites, -1)
    needed = jnp.any(wanted[:, :, None] == ids[None, None, :], axis=1)
    needed = needed.reshape(sites, sites, CB_DEV).astype(jnp.int32)
    lower = (jnp.arange(CB_DEV)[:, None] < jnp.arange(CB_DEV)[None, :]).astype(jnp.int32)
    rank = jnp.sum(needed[:, :, :, None] * lower[None, None], axis=2)
    slot_ids = jnp.arange(SLOTS, dtype=jnp.int32)
    chosen = (needed[..., None] == 1) & (rank[..., None] == slot_ids)
    local_ids = jnp.arange(CB_DEV, dtype=jnp.int32)
    table = jnp.sum(jnp.where(chosen, local_ids[:, None], 0), axis=2)

    def at(ex, ey):
        return ((x + ex) % n) * n + (y + ey) % n

    def picks(user, holders):
        return jnp.concatenate([table[user, h] for h in holders])

    lo, hi = transposed(normals)
    line = []
    for axis, own in ((0, lo), (1, hi)):
        below = step(own, axis, 1)
        above = step(own, axis, -1)
        line.append([own, above, None, below])
    for axis in (0, 1):
        _, above, _, below = line[axis]
        half = CB_DEV // 2
        far = [step(below[:half], axis, 1), step(above[half:], axis, -1)]
        line[axis][2] = jnp.concatenate(far, axis=0)
    near, rest = [], []
    for axis in (0, 1):
        near.append([])
        rest.append([])
        for d in range(1, n):
            user = at(0, d) if axis == 0 else at(d, 0)
            holders = [at(e, 0) if axis == 0 else at(0, e) for e in range(n)]
            p = jnp.take(line[axis][0], table[user, holders[0]], axis=0)
            near[axis].append(step(p, 1 - axis, d))
            q = jnp.concatenate(
                [jnp.take(line[axis][e], table[user, holders[e]], axis=0) for e in range(1, n)]
            )
            rest[axis].append(step(q, 1 - axis, d))

    own = jnp.concatenate([table[me, at(ex, ey)] for ex in range(n) for ey in range(n)])
    cols = lax.dynamic_slice_in_dim(pattern, me * RB_DEV, RB_DEV, 0).reshape(-1)
    holder = cols // CB_DEV
    ex = (holder // n - x) % n
    ey = (holder % n - y) % n
    my_rank = lax.dynamic_index_in_dim(rank, me, 0, keepdims=False).reshape(-1)
    slots = (ex * n + ey) * SLOTS + my_rank[cols]
    arrays = line[0] + line[1] + near[0] + rest[0] + near[1] + rest[1]
    rows = RB_DEV * BLK
    bus = lax.dynamic_slice_in_dim(bus_map, me * rows, rows, 0)
    shape = (RB_DEV, 1, BLK)
    power = main(
        slots, own, arrays, portion, temporal,
        capacity.reshape(shape), spread.reshape(shape), bus.reshape(shape), width,
    )
    tiles = lax.all_to_all(power.reshape(sites, -1, width), "site", 0, 0, tiled=True)
    return jnp.sum(tiles.astype(jnp.float32), axis=0)


def solution(mesh):
    placed = (P("site", "scen"), P(), P("site", None, "scen", None), P(), P("site"), P("site"), P())
    return jax.shard_map(
        shards, mesh=mesh, in_specs=placed, out_specs=P("site", "scen"), check_vma=False
    )
```

time: 325 us -> 289 us (0.89)
  blocking collectives: 116 us -> 21.4 us
  waiting for transfers between devices: 106 us -> 65.3 us
  other arithmetic: 22.7 us -> 58.2 us
  Pallas kernels: 0 us -> 32.2 us
  local copies, waits for them, and re-layouts: 41.3 us -> 69.3 us
  starting transfers between devices: 4.66 us -> 26.5 us
  matrix products: 19.5 us -> 0 us
    all_to_all x1 -> x0, waiting for transfers between devices: 106 us -> none  [exchange_in_pieces(): lax.all_to_all(piece, axis, split_axis=0, concat_axis=0, tiled=True)]
    all_to_all x2 -> x1, blocking collectives: 116 us -> 21.4 us  [shards(): lax.all_to_all(power.reshape(sites, -1, width), 'site', 0, 0, tiled=True)]
    ppermute x0 -> x20, waiting for transfers between devices: none -> 64.6 us  [shift(): return lax.ppermute(value, 'site', pairs)]
    pallas_call x0 -> x2, Pallas kernels: none -> 32.2 us  [the longest x1 25.4 us: main(): pl.pallas_call(main_kernel, grid_spec=grid_spec, out_shape=jax.ShapeDtype...]
    ppermute x0 -> x20, starting transfers between devices: none -> 26.5 us  [shift(): return lax.ppermute(value, 'site', pairs)]
    dot_general x3 -> x0, matrix products: 19.5 us -> none  [the longest x1 17.8 us: shards(): jnp.einsum('ktij,ktjw->kiw', portion, picked, preferred_element_type=jnp....]
    select_n x4 -> x43, other arithmetic: 7.76 us -> 27.1 us  [the longest x30 17.3 us: shards(): jnp.take(line[axis][e], table[user, holders[e]], axis=0)]
    gather x4 -> x25, local copies, waits for them, and re-layouts: 27.7 us -> 45.1 us  [the longest x18 34 us: shards(): jnp.take(line[axis][e], table[user, holders[e]], axis=0)]
  transfers between devices with their start and end apart: 2 -> 21, of which waited for: 1 -> 6; matrix products, arithmetic and copies ran while one was open for 19% -> 44% of each run, Pallas kernels for 0% -> 2%
where the time goes in v1:
time: 289 us; the launch traced here: 287 us
  local copies, waits for them, and re-layouts  69.3 us (24%)
  waiting for transfers between devices  65.3 us (23%)
  other arithmetic  58.2 us (20%)
  Pallas kernels  32.2 us (11%)
  starting transfers between devices  26.5 us (9%)
  blocking collectives  21.4 us (7%)
  between operations  14.2 us (5%)
    ppermute x20, waiting for transfers between devices, shift(): return lax.ppermute(value, 'site', pairs)  64.6 us
    gather x18, local copies, waits for them, and re-layouts, shards(): jnp.take(line[axis][e], table[user, holders[e]], axis=0)  34 us
    ppermute x20, starting transfers between devices, shift(): return lax.ppermute(value, 'site', pairs)  26.5 us
    pallas_call x1, Pallas kernels, main(): pl.pallas_call(main_kernel, grid_spec=grid_spec, out_shape=jax.ShapeDtype...  25.4 us
    all_to_all x1, blocking collectives, shards(): lax.all_to_all(power.reshape(sites, -1, width), 'site', 0, 0, tiled=True)  21.4 us
    select_n x30, other arithmetic, shards(): jnp.take(line[axis][e], table[user, holders[e]], axis=0)  17.3 us
    concatenate x6, other arithmetic, shards(): jnp.concatenate([jnp.take(line[axis][e], table[user, holders[e]], axis=0)...  12.2 us
    gather x6, local copies, waits for them, and re-layouts, shards(): p = jnp.take(line[axis][0], table[user, holders[0]], axis=0)  9.55 us
  transfers between devices with their start and end apart: 21, of which 6 were waited for; matrix products, arithmetic and copies ran while one was open for 44% of the time, Pallas kernels for 2%

profile of v1, /device:TPU:64, one launch (start us, length us, event | category | flops | bytes accessed | tf_op | source)
XLA Modules:
  0.0 287.1 jit_solution(3479673854128014599)
XLA Ops:
  8.0 2.4 copy.35.z_ref
  10.4 6.8 %shard_map.73 = (bf16[10,336,128]{2,1,0:T(8,128)(2,1)}, bf16[10,336,128]{2,1,0:T(8,128)(2,1)}) custom-call(bf16[2560,336]{1,0:T(8,128)(2,1)} %copy.35.z_ref), custom_call_target="tpu_custom_call" | custom-call | tf_op jit(solution)/shard_map/pallas_call | solution.py:45
  17.2 1.6 collective-permute-start.5
  18.8 1.7 collective-permute-start.4
  20.5 1.5 collective-permute-start.1
  21.9 1.7 collective-permute-start
  25.2 4.6 %fusion.40 = (s32[5]{0:T(128)S(1)}, s32[5]{0:T(128)S(1)}, s32[5]{0:T(128)S(1)}, s32[5]{0:T(128)S(1)}, s32[5]{0:T(128)S(1)}, /*index=5*/s32[5]{0:T(128)S(1)}, s32...) fusion(s32[16,16,5]{1,0,2:T(8,128)S(1)} %select_reduce_fusion, ...), kind=kLoop, calls=%fused_computation.198 | loop fusion | bytes 1668 | tf_op jit(solution)/shard_map/dynamic_slice | solution.py:204
  31.5 1.8 collective-permute-start.10
  33.3 1.8 gather_fusion.13
  35.1 2.6 gather_fusion.14
  39.4 1.2 compare_and_fusion.8
  40.6 1.3 compare_select_fusion.21
  41.9 1.3 compare_and_fusion.20
  47.5 1.2 compare_and_fusion.22
  51.6 1.3 compare_and_fusion.6
  56.9 2.6 gather_fusion.15
  59.5 1.4 gather_fusion.1
  62.2 1.9 broadcast_select_fusion.9
  64.1 1.9 broadcast_select_fusion.23
  68.3 1.8 slice.69
  70.1 1.4 gather_fusion.21
  71.5 2.6 gather_fusion.19
  74.1 1.4 gather_fusion.24
  75.4 2.5 gather_fusion.22
  78.0 1.4 gather_fusion.18
  79.4 1.8 gather_fusion.16
  81.2 3.1 %collective-permute-start.7 = (bf16[5,336,128]{2,1,0:T(8,128)(2,1)}, bf16[5,336,128]{2,1,0:T(8,128)(2,1)}, u32[]{:S(2)}, u32[]{:S(2)}) collective-permute-start(bf16[5,336,128]{2,1,0:T(8,128)(2,1)} %slice.69), channel_id=1, source_target_pairs={{0,24},{8,0},{16,8},{24,16},{32,56},{40,32},{48,40},{56,48},{64,88... | collective-permute-start | bytes 1290248 | tf_op jit(solution)/shard_map/ppermute | solution.py:27
  84.3 1.9 slice.66
  86.1 2.6 gather_fusion.12
  88.7 2.6 gather_fusion.9
  91.3 1.7 collective-permute-start.2
  93.0 1.4 gather_fusion.10
  94.4 1.4 gather_fusion.7
  95.8 2.5 gather_fusion.6
  99.2 1.9 broadcast_select_fusion.5
  111.4 2.8 collective-permute-start.15
  114.3 1.8 constant_dynamic-update-slice_fusion.3
  118.5 1.8 constant_dynamic-update-slice_fusion.2.refs_6_
  120.3 2.5 gather_fusion.20
  122.8 2.6 gather_fusion.23
  125.4 2.6 gather_fusion.17
  129.1 2.4 pad_maximum_fusion.4
  131.4 8.7 %collective-permute-done.3 = bf16[5,336,128]{2,1,0:T(8,128)(2,1)} collective-permute-done((bf16[5,336,128]{2,1,0:T(8,128)(2,1)}, bf16[5,336,128]{2,1,0:T(8,128)(2,1)}, u32[]{:S(2)}, u32[]{:S(2)}) %collective-permute-start.3) | collective-permute-done | bytes 430112 | tf_op jit(solution)/shard_map/ppermute | solution.py:27
  140.1 2.6 collective-permute-start.18
  143.8 1.4 gather_fusion.11
  146.3 2.5 pad_maximum_fusion.5
  149.9 1.2 pad_maximum_fusion.3
  151.1 1.4 gather_fusion.8
  152.5 2.6 pad_maximum_fusion.2
  155.3 1.8 collective-permute-start.9
  157.2 1.2 pad_maximum_fusion.1
  158.4 1.4 gather_fusion.5
  160.9 2.4 pad_maximum_fusion
  163.3 2.0 collective-permute-start.19
  165.3 11.2 %collective-permute-done.8.refs_8_ = bf16[5,336,128]{2,1,0:T(8,128)(2,1)} collective-permute-done((bf16[5,336,128]{2,1,0:T(8,128)(2,1)}, bf16[5,336,128]{2,1,0:T(8,128)(2,1)}, u32[]{:S(2)}, u32[]{:S(2)}) %collective-permute-start.8) | collective-permute-done | bytes 430112 | tf_op jit(solution)/shard_map/ppermute | solution.py:27
  177.1 1.5 collective-permute-start.11
  178.7 1.3 broadcast_divide_fusion
  184.2 1.6 gather_fusion
  188.0 11.0 %collective-permute-done.19.refs_19_ = bf16[15,336,128]{2,1,0:T(8,128)(2,1)} collective-permute-done((bf16[15,336,128]{2,1,0:T(8,128)(2,1)}, bf16[15,336,128]{2,1,0:T(8,128)(2,1)}, u32[]{:S(2)}, u32[]{:S(2)}) %collective-permute-start.19) | collective-permute-done | bytes 1290272 | tf_op jit(solution)/shard_map/ppermute | solution.py:27
  199.0 9.1 %collective-permute-done.13.refs_13_ = bf16[15,336,128]{2,1,0:T(8,128)(2,1)} collective-permute-done((bf16[15,336,128]{2,1,0:T(8,128)(2,1)}, bf16[15,336,128]{2,1,0:T(8,128)(2,1)}, u32[]{:S(2)}, u32[]{:S(2)}) %collective-permute-start.13) | collective-permute-done | bytes 1290272 | tf_op jit(solution)/shard_map/ppermute | solution.py:27
  208.1 1.5 collective-permute-done.12.refs_12_
  209.7 23.0 %collective-permute-done.11.refs_11_ = bf16[15,336,128]{2,1,0:T(8,128)(2,1)} collective-permute-done((bf16[15,336,128]{2,1,0:T(8,128)(2,1)}, bf16[15,336,128]{2,1,0:T(8,128)(2,1)}, u32[]{:S(2)}, u32[]{:S(2)}) %collective-permute-start.11) | collective-permute-done | bytes 1290272 | tf_op jit(solution)/shard_map/ppermute | solution.py:27
  232.7 25.4 %shard_map.74 = bf16[1024,336]{1,0:T(8,128)(2,1)S(1)} custom-call(s32[160]{0:T(256)S(1)} %multiply_add_fusion.slot_ref, s32[80]{0:T(128)S(1)} %concatenate.27.own_ref, bf16[10,336,128]{2,1,0:T(8,128)(2,1)S(1)} %copy-done, bf16[10,336,128]{2,1,0:T(8,128)(2,1)S(1)} %collective-permute-done.refs_1_, ...), custom_call_target="tpu_custom_call" | custom-call | tf_op jit(solution)/shard_map/pallas_call | solution.py:150
  258.1 21.4 %all_to_all.5 = bf16[16,64,336]{2,1,0:T(8,128)(2,1)S(1)} all-to-all(bf16[16,64,336]{2,1,0:T(8,128)(2,1)S(1)} %bitcast.5), channel_id=1, replica_groups=mesh['site'=16,'scen'=8] {'site'}, dimensions={0} | all-to-all | bytes 1376256 | tf_op jit(solution)/shard_map/all_to_all | solution.py:223
  (230 shorter events, 47.8 us)
Async XLA Ops:
  6.5 226.1 %all-gather.2.cloned.1.call-start = ((), (), s32[]{:S(2)}) async-start(), calls=%async_computation.1 | async-start | bytes 23592960 | tf_op jit(solution)/shard_map/all_gather | solution.py:164
  10.4 13.3 %copy-start.25 = (s32[64,40]{0,1:T(8,128)S(1)}, s32[64,40]{0,1:T(8,128)}, u32[]{:S(2)}) copy-start(s32[64,40]{0,1:T(8,128)} %param.10) | copy-start | bytes 30724
  17.2 12.7 %copy-start = (bf16[10,336,128]{2,1,0:T(8,128)(2,1)S(1)}, bf16[10,336,128]{2,1,0:T(8,128)(2,1)}, u32[]{:S(2)}) copy-start(bf16[10,336,128]{2,1,0:T(8,128)(2,1)} %get-tuple-element.8.refs_0_) | copy-start | bytes 2580484
  17.2 49.6 %collective-permute-start.5 = (bf16[10,336,128]{2,1,0:T(8,128)(2,1)}, bf16[10,336,128]{2,1,0:T(8,128)(2,1)S(1)}, u32[]{:S(2)}, u32[]{:S(2)}) collective-permute-start(bf16[10,336,128]{2,1,0:T(8,128)(2,1)} %get-tuple-element.9.refs_4_), channel_id=1, source_target_pairs={{0,8},{8,16},{16,24},{24,0},{32,40},{40,48},{48,56},{56,32},{64,72... | collective-permute-start | bytes 2580488 | tf_op jit(solution)/shard_map/ppermute | solution.py:27
  18.8 49.3 %collective-permute-start.4 = (bf16[10,336,128]{2,1,0:T(8,128)(2,1)}, bf16[10,336,128]{2,1,0:T(8,128)(2,1)}, u32[]{:S(2)}, u32[]{:S(2)}) collective-permute-start(bf16[10,336,128]{2,1,0:T(8,128)(2,1)} %get-tuple-element.9.refs_4_), channel_id=1, source_target_pairs={{0,24},{8,0},{16,8},{24,16},{32,56},{40,32},{48,40},{56,48},{64,88... | collective-permute-start | bytes 2580488 | tf_op jit(solution)/shard_map/ppermute | solution.py:27
  20.5 60.7 %collective-permute-start.1 = (bf16[10,336,128]{2,1,0:T(8,128)(2,1)}, bf16[10,336,128]{2,1,0:T(8,128)(2,1)}, u32[]{:S(2)}, u32[]{:S(2)}) collective-permute-start(bf16[10,336,128]{2,1,0:T(8,128)(2,1)} %get-tuple-element.8.refs_0_), channel_id=1, source_target_pairs={{0,32},{8,40},{16,48},{24,56},{32,64},{40,72},{48,80},{56,88},{64,... | collective-permute-start | bytes 2580488 | tf_op jit(solution)/shard_map/ppermute | solution.py:27
  21.9 69.3 %collective-permute-start = (bf16[10,336,128]{2,1,0:T(8,128)(2,1)}, bf16[10,336,128]{2,1,0:T(8,128)(2,1)S(1)}, u32[]{:S(2)}, u32[]{:S(2)}) collective-permute-start(bf16[10,336,128]{2,1,0:T(8,128)(2,1)} %get-tuple-element.8.refs_0_), channel_id=1, source_target_pairs={{0,96},{8,104},{16,112},{24,120},{32,0},{40,8},{48,16},{56,24},{64... | collective-permute-start | bytes 2580488 | tf_op jit(solution)/shard_map/ppermute | solution.py:27
  25.1 4.8 %copy-start.23 = (s32[16,16,10]{1,0,2:T(8,128)}, s32[16,16,10]{1,0,2:T(8,128)S(1)}, u32[]{:S(2)}) copy-start(s32[16,16,10]{1,0,2:T(8,128)S(1)} %multiply_reduce_fusion) | copy-start | bytes 30724
  29.8 5.3 %copy-start.45 = (s32[5]{0:T(128)}, s32[5]{0:T(128)S(1)}, u32[]{:S(2)}) copy-start(s32[5]{0:T(128)S(1)} %get-tuple-element.21) | copy-start | bytes 64
  29.8 5.3 %copy-start.44 = (s32[5]{0:T(128)}, s32[5]{0:T(128)S(1)}, u32[]{:S(2)}) copy-start(s32[5]{0:T(128)S(1)} %get-tuple-element.20) | copy-start | bytes 64
  29.8 7.9 %copy-start.28 = (s32[5]{0:T(128)}, s32[5]{0:T(128)S(1)}, u32[]{:S(2)}) copy-start(s32[5]{0:T(128)S(1)} %get-tuple-element.14) | copy-start | bytes 64
  29.8 7.9 %copy-start.27 = (s32[5]{0:T(128)}, s32[5]{0:T(128)S(1)}, u32[]{:S(2)}) copy-start(s32[5]{0:T(128)S(1)} %get-tuple-element.13) | copy-start | bytes 64
  29.8 7.9 %copy-start.29 = (s32[5]{0:T(128)}, s32[5]{0:T(128)S(1)}, u32[]{:S(2)}) copy-start(s32[5]{0:T(128)S(1)} %get-tuple-element.15) | copy-start | bytes 64
  29.9 8.0 %copy-start.34 = (s32[5]{0:T(128)}, s32[5]{0:T(128)S(1)}, u32[]{:S(2)}) copy-start(s32[5]{0:T(128)S(1)} %get-tuple-element.17) | copy-start | bytes 64
  29.9 8.0 %copy-start.33 = (s32[5]{0:T(128)}, s32[5]{0:T(128)S(1)}, u32[]{:S(2)}) copy-start(s32[5]{0:T(128)S(1)} %get-tuple-element.16) | copy-start | bytes 64
  29.9 8.0 %copy-start.46 = (s32[5]{0:T(128)}, s32[5]{0:T(128)S(1)}, u32[]{:S(2)}) copy-start(s32[5]{0:T(128)S(1)} %get-tuple-element.18) | copy-start | bytes 64
  29.9 8.2 %copy-start.32 = (s32[5]{0:T(128)}, s32[5]{0:T(128)S(1)}, u32[]{:S(2)}) copy-start(s32[5]{0:T(128)S(1)} %get-tuple-element.29) | copy-start | bytes 64
  29.9 8.2 %copy-start.31 = (s32[5]{0:T(128)}, s32[5]{0:T(128)S(1)}, u32[]{:S(2)}) copy-start(s32[5]{0:T(128)S(1)} %get-tuple-element.28) | copy-start | bytes 64
  31.5 123.8 %collective-permute-start.10 = (bf16[5,336,128]{2,1,0:T(8,128)(2,1)}, bf16[5,336,128]{2,1,0:T(8,128)(2,1)S(1)}, u32[]{:S(2)}, u32[]{:S(2)}) collective-permute-start(bf16[5,336,128]{2,1,0:T(8,128)(2,1)} %broadcast_select_fusion.21), channel_id=1, source_target_pairs={{0,24},{8,0},{16,8},{24,16},{32,56},{40,32},{48,40},{56,48},{64,88... | collective-permute-start | bytes 1290248 | tf_op jit(solution)/shard_map/ppermute | solution.py:27
  37.7 18.3 %copy-start.10 = (bf16[5,336,128]{2,1,0:T(8,128)(2,1)S(1)}, bf16[5,336,128]{2,1,0:T(8,128)(2,1)}, u32[]{:S(2)}) copy-start(bf16[5,336,128]{2,1,0:T(8,128)(2,1)} %gather_fusion.14) | copy-start | bytes 1290244
  59.5 4.6 %copy-start.48 = (pred[5]{0:T(512)(128)(4,1)S(1)}, pred[5]{0:T(512)(128)(4,1)}, u32[]{:S(2)}) copy-start(pred[5]{0:T(512)(128)(4,1)} %compare_and_fusion.23) | copy-start | bytes 19
  60.8 5.1 %copy-start.49 = (pred[5]{0:T(512)(128)(4,1)S(1)}, pred[5]{0:T(512)(128)(4,1)}, u32[]{:S(2)}) copy-start(pred[5]{0:T(512)(128)(4,1)} %compare_and_fusion.22) | copy-start | bytes 19
  66.8 11.1 %copy-start.4 = (bf16[10,336,128]{2,1,0:T(8,128)(2,1)}, bf16[10,336,128]{2,1,0:T(8,128)(2,1)S(1)}, u32[]{:S(2)}) copy-start(bf16[10,336,128]{2,1,0:T(8,128)(2,1)S(1)} %collective-permute-done.5.refs_7_) | copy-start | bytes 2580484
  66.8 88.5 %collective-permute-start.14 = (bf16[5,336,128]{2,1,0:T(8,128)(2,1)}, bf16[5,336,128]{2,1,0:T(8,128)(2,1)S(1)}, u32[]{:S(2)}, u32[]{:S(2)}) collective-permute-start(bf16[5,336,128]{2,1,0:T(8,128)(2,1)} %broadcast_select_fusion.11), channel_id=1, source_target_pairs={{0,32},{8,40},{16,48},{24,56},{32,64},{40,72},{48,80},{56,88},{64,... | collective-permute-start | bytes 1290248 | tf_op jit(solution)/shard_map/ppermute | solution.py:27
  68.1 43.4 %collective-permute-start.6 = (bf16[5,336,128]{2,1,0:T(8,128)(2,1)}, bf16[5,336,128]{2,1,0:T(8,128)(2,1)}, u32[]{:S(2)}, u32[]{:S(2)}) collective-permute-start(bf16[5,336,128]{2,1,0:T(8,128)(2,1)} %slice.68), channel_id=1, source_target_pairs={{0,8},{8,16},{16,24},{24,0},{32,40},{40,48},{48,56},{56,32},{64,72... | collective-permute-start | bytes 1290248 | tf_op jit(solution)/shard_map/ppermute | solution.py:27
  81.2 37.1 %collective-permute-start.7 = (bf16[5,336,128]{2,1,0:T(8,128)(2,1)}, bf16[5,336,128]{2,1,0:T(8,128)(2,1)}, u32[]{:S(2)}, u32[]{:S(2)}) collective-permute-start(bf16[5,336,128]{2,1,0:T(8,128)(2,1)} %slice.69), channel_id=1, source_target_pairs={{0,24},{8,0},{16,8},{24,16},{32,56},{40,32},{48,40},{56,48},{64,88... | collective-permute-start | bytes 1290248 | tf_op jit(solution)/shard_map/ppermute | solution.py:27
  91.3 7.1 %copy-start.15 = (bf16[5,336,128]{2,1,0:T(8,128)(2,1)S(1)}, bf16[5,336,128]{2,1,0:T(8,128)(2,1)}, u32[]{:S(2)}) copy-start(bf16[5,336,128]{2,1,0:T(8,128)(2,1)} %gather_fusion.21) | copy-start | bytes 1290244
  91.3 7.1 %copy-start.42 = (pred[5]{0:T(512)(128)(4,1)S(1)}, pred[5]{0:T(512)(128)(4,1)}, u32[]{:S(2)}) copy-start(pred[5]{0:T(512)(128)(4,1)} %get-tuple-element.67) | copy-start | bytes 19
  91.3 24.8 %collective-permute-start.2 = (bf16[5,336,128]{2,1,0:T(8,128)(2,1)}, bf16[5,336,128]{2,1,0:T(8,128)(2,1)}, u32[]{:S(2)}, u32[]{:S(2)}) collective-permute-start(bf16[5,336,128]{2,1,0:T(8,128)(2,1)} %slice.66), channel_id=1, source_target_pairs={{0,32},{8,40},{16,48},{24,56},{32,64},{40,72},{48,80},{56,88},{64,... | collective-permute-start | bytes 1290248 | tf_op jit(solution)/shard_map/ppermute | solution.py:27
  94.4 4.8 %copy-start.35 = (pred[5]{0:T(512)(128)(4,1)S(1)}, pred[5]{0:T(512)(128)(4,1)}, u32[]{:S(2)}) copy-start(pred[5]{0:T(512)(128)(4,1)} %get-tuple-element.69) | copy-start | bytes 19
  95.8 5.4 %copy-start.41 = (pred[5]{0:T(512)(128)(4,1)S(1)}, pred[5]{0:T(512)(128)(4,1)}, u32[]{:S(2)}) copy-start(pred[5]{0:T(512)(128)(4,1)} %get-tuple-element.64) | copy-start | bytes 19
  98.3 2.8 copy-start.14
  98.3 3.7 %copy-start.12 = (bf16[5,336,128]{2,1,0:T(8,128)(2,1)S(1)}, bf16[5,336,128]{2,1,0:T(8,128)(2,1)}, u32[]{:S(2)}) copy-start(bf16[5,336,128]{2,1,0:T(8,128)(2,1)} %gather_fusion.22) | copy-start | bytes 1290244
  98.3 3.7 %copy-start.36 = (pred[5]{0:T(512)(128)(4,1)S(1)}, pred[5]{0:T(512)(128)(4,1)}, u32[]{:S(2)}) copy-start(pred[5]{0:T(512)(128)(4,1)} %get-tuple-element.66) | copy-start | bytes 19
  99.2 3.7 %copy-start.11 = (bf16[5,336,128]{2,1,0:T(8,128)(2,1)S(1)}, bf16[5,336,128]{2,1,0:T(8,128)(2,1)}, u32[]{:S(2)}) copy-start(bf16[5,336,128]{2,1,0:T(8,128)(2,1)} %gather_fusion.18) | copy-start | bytes 1290244
  99.2 3.7 %copy-start.38 = (pred[5]{0:T(512)(128)(4,1)S(1)}, pred[5]{0:T(512)(128)(4,1)}, u32[]{:S(2)}) copy-start(pred[5]{0:T(512)(128)(4,1)} %get-tuple-element.70) | copy-start | bytes 19
  101.2 2.7 copy-start.47
  102.0 2.7 copy-start.16
  102.0 2.7 copy-start.37
  102.9 2.7 copy-start.20
  102.9 2.7 copy-start.39
  103.8 2.7 copy-start.13
  104.7 2.7 copy-start.18
  105.6 2.6 copy-start.17
  105.6 2.6 copy-start.40
  111.4 51.8 %collective-permute-start.15 = (bf16[5,336,128]{2,1,0:T(8,128)(2,1)}, bf16[5,336,128]{2,1,0:T(8,128)(2,1)}, u32[]{:S(2)}, u32[]{:S(2)}) collective-permute-start(bf16[5,336,128]{2,1,0:T(8,128)(2,1)} %broadcast_select_fusion.10), channel_id=1, source_target_pairs={{0,64},{8,72},{16,80},{24,88},{32,96},{40,104},{48,112},{56,120},{... | collective-permute-start | bytes 1290248 | tf_op jit(solution)/shard_map/ppermute | solution.py:27
  116.1 49.2 %collective-permute-start.16 = (bf16[5,336,128]{2,1,0:T(8,128)(2,1)}, bf16[5,336,128]{2,1,0:T(8,128)(2,1)}, u32[]{:S(2)}, u32[]{:S(2)}) collective-permute-start(bf16[5,336,128]{2,1,0:T(8,128)(2,1)} %broadcast_select_fusion.9), channel_id=1, source_target_pairs={{0,96},{8,104},{16,112},{24,120},{32,0},{40,8},{48,16},{56,24},{64... | collective-permute-start | bytes 1290248 | tf_op jit(solution)/shard_map/ppermute | solution.py:27
  118.3 21.8 %collective-permute-start.3 = (bf16[5,336,128]{2,1,0:T(8,128)(2,1)}, bf16[5,336,128]{2,1,0:T(8,128)(2,1)}, u32[]{:S(2)}, u32[]{:S(2)}) collective-permute-start(bf16[5,336,128]{2,1,0:T(8,128)(2,1)} %slice.67), channel_id=1, source_target_pairs={{0,96},{8,104},{16,112},{24,120},{32,0},{40,8},{48,16},{56,24},{64... | collective-permute-start | bytes 1290248 | tf_op jit(solution)/shard_map/ppermute | solution.py:27
  120.3 7.7 %copy-start.30 = (pred[5]{0:T(512)(128)(4,1)S(1)}, pred[5]{0:T(512)(128)(4,1)}, u32[]{:S(2)}) copy-start(pred[5]{0:T(512)(128)(4,1)} %get-tuple-element.68) | copy-start | bytes 19
  140.1 37.0 %collective-permute-start.18 = (bf16[15,336,128]{2,1,0:T(8,128)(2,1)}, bf16[15,336,128]{2,1,0:T(8,128)(2,1)}, u32[]{:S(2)}, u32[]{:S(2)}) collective-permute-start(bf16[15,336,128]{2,1,0:T(8,128)(2,1)} %pad_maximum_fusion.4), channel_id=1, source_target_pairs={{0,64},{8,72},{16,80},{24,88},{32,96},{40,104},{48,112},{56,120},{... | collective-permute-start | bytes 3870728 | tf_op jit(solution)/shard_map/ppermute | solution.py:27
  146.3 2.6 copy-start.21
  152.5 2.6 copy-start.22
  152.5 4.7 %copy-start.6 = (bf16[5,336,128]{2,1,0:T(8,128)(2,1)S(1)}, bf16[5,336,128]{2,1,0:T(8,128)(2,1)}, u32[]{:S(2)}) copy-start(bf16[5,336,128]{2,1,0:T(8,128)(2,1)} %broadcast_select_fusion.15) | copy-start | bytes 1290244
  152.5 4.7 %copy-start.7 = (bf16[5,336,128]{2,1,0:T(8,128)(2,1)S(1)}, bf16[5,336,128]{2,1,0:T(8,128)(2,1)}, u32[]{:S(2)}) copy-start(bf16[5,336,128]{2,1,0:T(8,128)(2,1)} %broadcast_select_fusion.17) | copy-start | bytes 1290244
  155.3 21.3 %collective-permute-start.8 = (bf16[5,336,128]{2,1,0:T(8,128)(2,1)}, bf16[5,336,128]{2,1,0:T(8,128)(2,1)}, u32[]{:S(2)}, u32[]{:S(2)}) collective-permute-start(bf16[5,336,128]{2,1,0:T(8,128)(2,1)} %broadcast_select_fusion.23), channel_id=1, source_target_pairs={{0,8},{8,16},{16,24},{24,0},{32,40},{40,48},{48,56},{56,32},{64,72... | collective-permute-start | bytes 1290248 | tf_op jit(solution)/shard_map/ppermute | solution.py:27
  155.3 21.2 %collective-permute-start.9 = (bf16[5,336,128]{2,1,0:T(8,128)(2,1)}, bf16[5,336,128]{2,1,0:T(8,128)(2,1)}, u32[]{:S(2)}, u32[]{:S(2)}) collective-permute-start(bf16[5,336,128]{2,1,0:T(8,128)(2,1)} %broadcast_select_fusion.22), channel_id=1, source_target_pairs={{0,16},{8,24},{16,0},{24,8},{32,48},{40,56},{48,32},{56,40},{64,80... | collective-permute-start | bytes 1290248 | tf_op jit(solution)/shard_map/ppermute | solution.py:27
  160.9 71.8 %copy-start.1 = (bf16[168,168]{1,0:T(8,128)(2,1)S(1)}, bf16[168,168]{1,0:T(8,128)(2,1)}, u32[]{:S(2)}) copy-start(bf16[168,168]{1,0:T(8,128)(2,1)} %refs_21_.1) | copy-start | bytes 169348
  160.9 71.8 %copy-start.2 = (f32[1024]{0:T(1024)S(1)}, f32[1024]{0:T(1024)}, u32[]{:S(2)}) copy-start(f32[1024]{0:T(1024)} %param.13) | copy-start | bytes 12292
  160.9 71.8 %copy-start.3 = (f32[1024]{0:T(1024)S(1)}, f32[1024]{0:T(1024)}, u32[]{:S(2)}) copy-start(f32[1024]{0:T(1024)} %param.14) | copy-start | bytes 12292
  163.3 35.8 %collective-permute-start.19 = (bf16[15,336,128]{2,1,0:T(8,128)(2,1)}, bf16[15,336,128]{2,1,0:T(8,128)(2,1)}, u32[]{:S(2)}, u32[]{:S(2)}) collective-permute-start(bf16[15,336,128]{2,1,0:T(8,128)(2,1)} %pad_maximum_fusion.5), channel_id=1, source_target_pairs={{0,96},{8,104},{16,112},{24,120},{32,0},{40,8},{48,16},{56,24},{64... | collective-permute-start | bytes 3870728 | tf_op jit(solution)/shard_map/ppermute | solution.py:27
  165.3 33.7 %collective-permute-start.17 = (bf16[15,336,128]{2,1,0:T(8,128)(2,1)}, bf16[15,336,128]{2,1,0:T(8,128)(2,1)}, u32[]{:S(2)}, u32[]{:S(2)}) collective-permute-start(bf16[15,336,128]{2,1,0:T(8,128)(2,1)} %pad_maximum_fusion.3), channel_id=1, source_target_pairs={{0,32},{8,40},{16,48},{24,56},{32,64},{40,72},{48,80},{56,88},{64,... | collective-permute-start | bytes 3870728 | tf_op jit(solution)/shard_map/ppermute | solution.py:27
  176.6 31.6 %collective-permute-start.13 = (bf16[15,336,128]{2,1,0:T(8,128)(2,1)}, bf16[15,336,128]{2,1,0:T(8,128)(2,1)}, u32[]{:S(2)}, u32[]{:S(2)}) collective-permute-start(bf16[15,336,128]{2,1,0:T(8,128)(2,1)} %pad_maximum_fusion.2), channel_id=1, source_target_pairs={{0,24},{8,0},{16,8},{24,16},{32,56},{40,32},{48,40},{56,48},{64,88... | collective-permute-start | bytes 3870728 | tf_op jit(solution)/shard_map/ppermute | solution.py:27
  176.6 33.1 %collective-permute-start.12 = (bf16[15,336,128]{2,1,0:T(8,128)(2,1)}, bf16[15,336,128]{2,1,0:T(8,128)(2,1)}, u32[]{:S(2)}, u32[]{:S(2)}) collective-permute-start(bf16[15,336,128]{2,1,0:T(8,128)(2,1)} %pad_maximum_fusion.1), channel_id=1, source_target_pairs={{0,16},{8,24},{16,0},{24,8},{32,48},{40,56},{48,32},{56,40},{64,80... | collective-permute-start | bytes 3870728 | tf_op jit(solution)/shard_map/ppermute | solution.py:27
  177.1 55.5 %collective-permute-start.11 = (bf16[15,336,128]{2,1,0:T(8,128)(2,1)}, bf16[15,336,128]{2,1,0:T(8,128)(2,1)}, u32[]{:S(2)}, u32[]{:S(2)}) collective-permute-start(bf16[15,336,128]{2,1,0:T(8,128)(2,1)} %pad_maximum_fusion), channel_id=1, source_target_pairs={{0,8},{8,16},{16,24},{24,0},{32,40},{40,48},{48,56},{56,32},{64,72... | collective-permute-start | bytes 3870728 | tf_op jit(solution)/shard_map/ppermute | solution.py:27
  (7 other events, 10.4 us)
Sparse Core Ops, SparseCore 0:
  9.1 103.8 all-gather.1

commit v2 on v1

v2 whole, which is shorter than its diff:
```python
import functools

import jax
import jax.numpy as jnp
from jax import lax
from jax.experimental import pallas as pl
from jax.experimental.pallas import tpu as pltpu
from jax.sharding import PartitionSpec as P

BLK = 256
HALF = 128
HOURS = 168
NZ = 40
SLOTS = 5
RB_DEV = 4
CB_DEV = 10
SIDE = 4
BUSES = 1024
COLS = 160


def shift(value, dx, dy):
    n = SIDE
    pairs = [
        (x * n + y, ((x + dx) % n) * n + (y + dy) % n) for x in range(n) for y in range(n)
    ]
    return lax.ppermute(value, "site", pairs)


def step(value, axis, d):
    return shift(value, d, 0) if axis == 0 else shift(value, 0, d)


def wait_all(copies):
    for c in copies:
        c.start()
    for c in copies:
        c.wait()


def after(value, *others):
    return lax.optimization_barrier((value, *others))[0]


def reblock_kernel(z_ref, lo_ref, hi_ref, sem):
    copies = []
    for b in range(CB_DEV):
        for h, out in enumerate((lo_ref, hi_ref)):
            src = z_ref.at[:, pl.ds(b * BLK + h * HALF, HALF)]
            copies.append(pltpu.make_async_copy(src, out.at[b], sem))
    wait_all(copies)


def reblocked(normals_t):
    width = normals_t.shape[0]
    out = jax.ShapeDtypeStruct((CB_DEV, width, HALF), normals_t.dtype)
    any_spec = pl.BlockSpec(memory_space=pl.ANY)
    return pl.pallas_call(
        reblock_kernel,
        in_specs=[any_spec],
        out_specs=[pl.BlockSpec(memory_space=pltpu.VMEM)] * 2,
        out_shape=[out, out],
        scratch_shapes=[pltpu.SemaphoreType.DMA],
    )(normals_t)


def device_at(x, y, ex, ey):
    return lax.rem(x + ex, SIDE) * SIDE + lax.rem(y + ey, SIDE)


def pick_kernel(hops, holders, me_ref, table_ref, *refs):
    count = len(holders)
    lines, outs, sem = (refs[:count], refs[count : 2 * count]), refs[2 * count : -1], refs[-1]
    x, y = me_ref[0] // SIDE, lax.rem(me_ref[0], SIDE)
    copies = []
    for axis in (0, 1):
        for k, d in enumerate(hops):
            user = device_at(x, y, 0, d) if axis == 0 else device_at(x, y, d, 0)
            out = outs[axis * len(hops) + k]
            for i, e in enumerate(holders):
                holder = device_at(x, y, e, 0) if axis == 0 else device_at(x, y, 0, e)
                for s in range(SLOTS):
                    local = table_ref[(user * SIDE * SIDE + holder) * SLOTS + s]
                    src = lines[axis][i].at[local]
                    copies.append(pltpu.make_async_copy(src, out.at[i * SLOTS + s], sem))
    wait_all(copies)


def picked(hops, holders, scalars, lines):
    width = lines[0][0].shape[1]
    out = jax.ShapeDtypeStruct((len(holders) * SLOTS, width, HALF), lines[0][0].dtype)
    outs = 2 * len(hops)
    return pl.pallas_call(
        functools.partial(pick_kernel, hops, holders),
        grid_spec=pltpu.PrefetchScalarGridSpec(
            num_scalar_prefetch=2,
            grid=(),
            in_specs=[pl.BlockSpec(memory_space=pl.ANY)] * (2 * len(holders)),
            out_specs=[pl.BlockSpec(memory_space=pltpu.VMEM)] * outs,
            scratch_shapes=[pltpu.SemaphoreType.DMA],
        ),
        out_shape=[out] * outs,
        compiler_params=pltpu.CompilerParams(vmem_limit_bytes=32 << 20),
    )(*scalars, *[lines[axis][e] for axis in (0, 1) for e in holders])


def slots_of(ex, ey):
    return (ex * SIDE + ey) * SLOTS


def main_kernel(me_ref, table_ref, rank_ref, cols_ref, *refs):
    lo_line, hi_line = refs[0:4], refs[4:8]
    sent = {(0, 1): refs[8], (0, 3): refs[9], (1, 1): refs[10], (1, 3): refs[11]}
    last = {(0, 1): refs[12], (0, 3): refs[13], (1, 1): refs[14], (1, 3): refs[15]}
    opposite = refs[16:18]
    f_ref, temporal_ref, cap_ref, spr_ref, bus_ref, out_ref, zlo, zhi, power, sem = refs[18:]

    def arrived(axis, d, e, s):
        if d == 2:
            return opposite[axis].at[e * SLOTS + s]
        if e == 2:
            return last[axis, d].at[s]
        return sent[axis, d].at[(e - e // 3) * SLOTS + s]

    r = pl.program_id(0)
    me = me_ref[0]
    x, y = me // SIDE, lax.rem(me, SIDE)

    def slot_at(t):
        col = cols_ref[(me * RB_DEV + r) * NZ + t]
        holder = col // CB_DEV
        ex = lax.rem(holder // SIDE - x + SIDE, SIDE)
        ey = lax.rem(lax.rem(holder, SIDE) - y + SIDE, SIDE)
        return slots_of(ex, ey) + rank_ref[me * COLS + col]

    def copies(fn):
        for ex in range(SIDE):
            for ey in range(SIDE):
                base = slots_of(ex, ey)
                holder = device_at(x, y, ex, ey)
                for s in range(SLOTS):
                    local = table_ref[(me * SIDE * SIDE + holder) * SLOTS + s]
                    if ey == 0:
                        src = lo_line[ex].at[local]
                    else:
                        src = arrived(0, SIDE - ey, ex, s)
                    fn(pltpu.make_async_copy(src, zlo.at[base + s], sem))
                    if ex == 0:
                        src = hi_line[ey].at[local]
                    else:
                        src = arrived(1, SIDE - ex, ey, s)
                    fn(pltpu.make_async_copy(src, zhi.at[base + s], sem))

    @pl.when(r == 0)
    def _():
        copies(lambda d: d.start())
        power[...] = jnp.zeros_like(power)
        copies(lambda d: d.wait())

    total = None
    for t in range(NZ):
        slot = slot_at(t)
        z = jnp.concatenate([zlo[slot], zhi[slot]], axis=1)
        term = lax.dot_general(
            z, f_ref[0, t], (((1,), (1,)), ((), ())), preferred_element_type=jnp.float32
        )
        total = term if total is None else total + term
    cap, spr = cap_ref[0], spr_ref[0]
    parts = []
    for s in range(total.shape[0] // HOURS):
        spatial = total[s * HOURS : (s + 1) * HOURS].astype(jnp.bfloat16)
        weather = jnp.dot(temporal_ref[...], spatial, preferred_element_type=jnp.float32)
        parts.append(cap * jnp.exp(spr * weather - 0.5 * spr * spr))
    injected = jnp.concatenate(parts, axis=0).astype(jnp.bfloat16)
    buses = lax.broadcasted_iota(jnp.int32, (BUSES, BLK), 0)
    onehot = jnp.where(buses == bus_ref[0], 1.0, 0.0).astype(jnp.bfloat16)
    power[...] += lax.dot_general(
        onehot, injected, (((1,), (1,)), ((), ())), preferred_element_type=jnp.float32
    )

    @pl.when(r == pl.num_programs(0) - 1)
    def _():
        out_ref[...] = power[...].astype(jnp.bfloat16)


def main(scalars, arrays, factor, temporal, cap, spr, bus, width):
    any_spec = pl.BlockSpec(memory_space=pltpu.HBM)
    vec = pl.BlockSpec((1, 1, BLK), lambda r, *_: (r, 0, 0))
    grid_spec = pltpu.PrefetchScalarGridSpec(
        num_scalar_prefetch=len(scalars),
        grid=(RB_DEV,),
        in_specs=[any_spec] * len(arrays)
        + [
            pl.BlockSpec((1, NZ, BLK, BLK), lambda r, *_: (r, 0, 0, 0)),
            pl.BlockSpec((HOURS, HOURS), lambda r, *_: (0, 0)),
            vec,
            vec,
            vec,
        ],
        out_specs=pl.BlockSpec((BUSES, width), lambda r, *_: (0, 0)),
        scratch_shapes=[
            pltpu.VMEM((SIDE * SIDE * SLOTS, width, HALF), jnp.bfloat16),
            pltpu.VMEM((SIDE * SIDE * SLOTS, width, HALF), jnp.bfloat16),
            pltpu.VMEM((BUSES, width), jnp.float32),
            pltpu.SemaphoreType.DMA,
        ],
    )
    return pl.pallas_call(
        main_kernel,
        grid_spec=grid_spec,
        out_shape=jax.ShapeDtypeStruct((BUSES, width), jnp.bfloat16),
        compiler_params=pltpu.CompilerParams(vmem_limit_bytes=48 << 20),
        cost_estimate=pl.CostEstimate(
            flops=2 * RB_DEV * NZ * BLK * BLK * width,
            bytes_accessed=36 << 20,
            transcendentals=RB_DEV * BLK * width,
        ),
    )(*scalars, *arrays, factor, temporal, cap, spr, bus)


def shards(normals, pattern, factor, temporal, capacity, spread, bus_map):
    width = normals.shape[1]
    n = SIDE
    sites = n * n
    me = lax.axis_index("site")
    portion = lax.all_gather(factor, "scen", axis=2, tiled=True)

    ids = jnp.arange(sites * CB_DEV, dtype=jnp.int32)
    wanted = pattern.reshape(sites, -1)
    needed = jnp.any(wanted[:, :, None] == ids[None, None, :], axis=1)
    needed = needed.reshape(sites, sites, CB_DEV).astype(jnp.int32)
    lower = (jnp.arange(CB_DEV)[:, None] < jnp.arange(CB_DEV)[None, :]).astype(jnp.int32)
    rank = jnp.sum(needed[:, :, :, None] * lower[None, None], axis=2)
    slot_ids = jnp.arange(SLOTS, dtype=jnp.int32)
    chosen = (needed[..., None] == 1) & (rank[..., None] == slot_ids)
    local_ids = jnp.arange(CB_DEV, dtype=jnp.int32)
    table = jnp.sum(jnp.where(chosen, local_ids[:, None], 0), axis=2)

    table = table.reshape(-1)
    index = me.reshape(1).astype(jnp.int32)

    lo, hi = reblocked(normals.T)
    lines = [[lo, None, None, None], [hi, None, None, None]]
    ring = [(axis, e) for axis in (0, 1) for e in (1, 3)]
    for axis, e in ring:
        lines[axis][e] = step(lines[axis][0], axis, -e)
    first = [lines[axis][e] for axis, e in ring]
    lines[0][2] = step(after(lo, *first), 0, 2)
    lines[1][2] = step(after(hi, *first), 1, 2)
    second = [lines[0][2], lines[1][2]]
    tables = (index, table)
    out = picked((1, 3), (0, 1, 3), tables, lines)
    sent = [step(after(b, *second), 1 - axis, d) for b, (axis, d) in zip(out, ring)]
    out = picked((2,), (0, 1, 2, 3), tables, lines)
    opposite = [step(after(b, *sent), 1 - axis, 2) for axis, b in enumerate(out)]
    out = picked((1, 3), (2,), tables, lines)
    last = [step(after(b, *opposite), 1 - axis, d) for b, (axis, d) in zip(out, ring)]
    arrays = lines[0] + lines[1] + sent + last + opposite
    scalars = (index, table, rank.reshape(-1), pattern.reshape(-1))
    rows = RB_DEV * BLK
    bus = lax.dynamic_slice_in_dim(bus_map, me * rows, rows, 0)
    shape = (RB_DEV, 1, BLK)
    power = main(
        scalars, arrays, portion, temporal,
        capacity.reshape(shape), spread.reshape(shape), bus.reshape(shape), width,
    )
    tiles = lax.all_to_all(power.reshape(sites, -1, width), "site", 0, 0, tiled=True)
    return jnp.sum(tiles.astype(jnp.float32), axis=0)


def solution(mesh):
    placed = (P("site", "scen"), P(), P("site", None, "scen", None), P(), P("site"), P("site"), P())
    return jax.shard_map(
        shards, mesh=mesh, in_specs=placed, out_specs=P("site", "scen"), check_vma=False
    )
```

time: 289 us -> 197 us (0.68)
  other arithmetic: 58.2 us -> 3.1 us
  local copies, waits for them, and re-layouts: 69.3 us -> 16.3 us
  Pallas kernels: 32.2 us -> 40.7 us
  starting transfers between devices: 26.5 us -> 34.8 us
  waiting for transfers between devices: 65.3 us -> 70.1 us
  blocking collectives: 21.4 us -> 16.8 us
    gather x25 -> x0, local copies, waits for them, and re-layouts: 45.1 us -> none  [the longest x18 34 us: shards(): jnp.take(line[axis][e], table[user, holders[e]], axis=0)]
    select_n x43 -> x0, other arithmetic: 27.1 us -> none  [the longest x30 17.3 us: shards(): jnp.take(line[axis][e], table[user, holders[e]], axis=0)]
    and x17 -> x0, other arithmetic: 14.5 us -> none  [the longest x10 8.92 us: shards(): jnp.take(line[axis][e], table[user, holders[e]], axis=0)]
    pallas_call x1 -> x4, Pallas kernels: 6.79 us -> 19.5 us  [the longest x3 16.7 us: picked(): pl.pallas_call(functools.partial(pick_kernel, hops, holders), grid_spec=p...]
    concatenate x6 -> x0, other arithmetic: 12.2 us -> none  [shards(): jnp.concatenate([jnp.take(line[axis][e], table[user, holders[e]], axis=0)...]
    ppermute x20 -> x16, starting transfers between devices: 26.5 us -> 34.8 us  [shift(): return lax.ppermute(value, 'site', pairs)]
    dynamic_slice x3 -> x0, local copies, waits for them, and re-layouts: 5.46 us -> none  [the longest x1 4.59 us: shards(): table[user, holders[e]]]
    slice x4 -> x0, local copies, waits for them, and re-layouts: 5.26 us -> none  [shards(): far = [step(below[:half], axis, 1), step(above[half:], axis, -1)]]
  transfers between devices with their start and end apart: 21 -> 17, of which waited for: 6 -> 12; matrix products, arithmetic and copies ran while one was open for 44% -> 6% of each run, Pallas kernels for 2% -> 10%
where the time goes in v2:
time: 197 us; the launch traced here: 195 us
  waiting for transfers between devices  70.1 us (36%)
  Pallas kernels  40.7 us (21%)
  starting transfers between devices  34.8 us (18%)
  blocking collectives  16.8 us (9%)
  local copies, waits for them, and re-layouts  16.3 us (8%)
  between operations  13.6 us (7%)
  other arithmetic  3.1 us (2%)
    ppermute x16, waiting for transfers between devices, shift(): return lax.ppermute(value, 'site', pairs)  69.4 us
    ppermute x16, starting transfers between devices, shift(): return lax.ppermute(value, 'site', pairs)  34.8 us
    pallas_call x1, Pallas kernels, main(): pl.pallas_call(main_kernel, grid_spec=grid_spec, out_shape=jax.ShapeDtype...  21.2 us
    all_to_all x1, blocking collectives, shards(): lax.all_to_all(power.reshape(sites, -1, width), 'site', 0, 0, tiled=True)  16.8 us
    pallas_call x3, Pallas kernels, picked(): pl.pallas_call(functools.partial(pick_kernel, hops, holders), grid_spec=p...  16.7 us
    unnamed x37, local copies, waits for them, and re-layouts  6.66 us
  transfers between devices with their start and end apart: 17, of which 12 were waited for; matrix products, arithmetic and copies ran while one was open for 6% of the time, Pallas kernels for 10%

profile of v2, /device:TPU:64, one launch (start us, length us, event | category | flops | bytes accessed | tf_op | source)
XLA Modules:
  0.0 195.4 jit_solution(12995490276206798260)
XLA Ops:
  6.5 0.7 all-gather.2.cloned.1.call-update
  7.3 2.8 %shard_map.73 = (bf16[10,336,128]{2,1,0:T(8,128)(2,1)}, bf16[10,336,128]{2,1,0:T(8,128)(2,1)}) custom-call(bf16[336,2560]{1,0:T(8,128)(2,1)} %bitcast.10), custom_call_target="tpu_custom_call" | custom-call | tf_op jit(solution)/shard_map/pallas_call | solution.py:58
  10.0 2.8 %collective-permute-start = (bf16[10,336,128]{2,1,0:T(8,128)(2,1)}, bf16[10,336,128]{2,1,0:T(8,128)(2,1)S(1)}, u32[]{:S(2)}, u32[]{:S(2)}) collective-permute-start(bf16[10,336,128]{2,1,0:T(8,128)(2,1)} %get-tuple-element.31.refs_0_), channel_id=1, source_target_pairs={{0,96},{8,104},{16,112},{24,120},{32,0},{40,8},{48,16},{56,24},{64... | collective-permute-start | bytes 2580488 | tf_op jit(solution)/shard_map/ppermute | solution.py:27
  12.9 0.0 collective-permute-start.1
  12.9 3.0 %collective-permute-start.2 = (bf16[10,336,128]{2,1,0:T(8,128)(2,1)}, bf16[10,336,128]{2,1,0:T(8,128)(2,1)S(1)}, u32[]{:S(2)}, u32[]{:S(2)}) collective-permute-start(bf16[10,336,128]{2,1,0:T(8,128)(2,1)} %get-tuple-element.32.refs_3_.refs_4_), channel_id=1, source_target_pairs={{0,24},{8,0},{16,8},{24,16},{32,56},{40,32},{48,40},{56,48},{64,88... | collective-permute-start | bytes 2580488 | tf_op jit(solution)/shard_map/ppermute | solution.py:27
  15.9 0.0 collective-permute-start.3
  15.9 15.7 %collective-permute-done.refs_1_ = bf16[10,336,128]{2,1,0:T(8,128)(2,1)S(1)} collective-permute-done((bf16[10,336,128]{2,1,0:T(8,128)(2,1)}, bf16[10,336,128]{2,1,0:T(8,128)(2,1)S(1)}, u32[]{:S(2)}, u32[]{:S(2)}) %collective-permute-start) | collective-permute-done | bytes 860192 | tf_op jit(solution)/shard_map/ppermute | solution.py:27
  31.6 3.3 %collective-permute-done.1.refs_2_.refs_3_ = bf16[10,336,128]{2,1,0:T(8,128)(2,1)S(1)} collective-permute-done((bf16[10,336,128]{2,1,0:T(8,128)(2,1)}, bf16[10,336,128]{2,1,0:T(8,128)(2,1)S(1)}, u32[]{:S(2)}, u32[]{:S(2)}) %collective-permute-start.1) | collective-permute-done | bytes 860192 | tf_op jit(solution)/shard_map/ppermute | solution.py:27
  34.9 2.7 %collective-permute-done.3.refs_5_.refs_7_ = bf16[10,336,128]{2,1,0:T(8,128)(2,1)S(1)} collective-permute-done((bf16[10,336,128]{2,1,0:T(8,128)(2,1)}, bf16[10,336,128]{2,1,0:T(8,128)(2,1)S(1)}, u32[]{:S(2)}, u32[]{:S(2)}) %collective-permute-start.3) | collective-permute-done | bytes 860192 | tf_op jit(solution)/shard_map/ppermute | solution.py:27
  37.6 0.9 copy-done.3
  38.5 0.5 collective-permute-start.5
  39.0 1.5 collective-permute-start.4
  40.5 0.1 copy.10
  40.6 0.1 eq.39
  40.7 0.5 fusion
  41.2 0.0 copy-done.16
  41.2 0.8 reshape.60
  42.0 1.1 copy.12
  43.1 1.5 broadcast_compare_fusion
  44.6 0.9 copy.11
  45.5 0.2 multiply_reduce_fusion
  45.7 0.0 copy-start.15
  45.7 0.6 copy-done.15
  46.4 0.1 select_reduce_fusion
  46.5 0.8 copy.13
  47.3 1.1 reshape.53.table_ref
  48.4 1.2 copy-done.1
  49.7 1.2 copy-done.4
  50.8 8.5 %shard_map.74 = (bf16[15,336,128]{2,1,0:T(8,128)(2,1)S(1)}, bf16[15,336,128]{2,1,0:T(8,128)(2,1)S(1)}, bf16[15,336,128]{2,1,0:T(8,128)(2,1)S(1)}, bf16[15,336,128]{2,1,0:T(8,128)(2,1)S(1)}) custom-call(s32[1]{0:T(128)} %bitcast.me_ref, s32[1280]{0:T(1024)S(1)} %reshape.53.table_ref, bf16[10,336,128]{2,1,0:T(8,128)(2,1)S(1)} %copy-done, ...), custom_call_target="tpu_custom_call" | custom-call | tf_op jit(solution)/shard_map/pallas_call | solution.py:93
  59.4 0.3 collective-permute-done.5.refs_1_.refs_6_
  59.7 0.5 collective-permute-done.4.refs_0_.refs_2_
  60.2 2.2 %collective-permute-start.9 = (bf16[15,336,128]{2,1,0:T(8,128)(2,1)S(1)}, bf16[15,336,128]{2,1,0:T(8,128)(2,1)S(1)}, u32[]{:S(2)}, u32[]{:S(2)}) collective-permute-start(bf16[15,336,128]{2,1,0:T(8,128)(2,1)S(1)} %get-tuple-element.40), channel_id=1, source_target_pairs={{0,96},{8,104},{16,112},{24,120},{32,0},{40,8},{48,16},{56,24},{64... | collective-permute-start | bytes 3870728 | tf_op jit(solution)/shard_map/ppermute | solution.py:27
  62.4 0.0 collective-permute-start.8
  62.4 1.9 collective-permute-start.7
  64.3 0.1 collective-permute-start.6
  64.4 4.8 %shard_map.76 = (bf16[20,336,128]{2,1,0:T(8,128)(2,1)S(1)}, bf16[20,336,128]{2,1,0:T(8,128)(2,1)S(1)}) custom-call(s32[1]{0:T(128)} %bitcast.me_ref, s32[1280]{0:T(1024)S(1)} %reshape.53.table_ref, bf16[10,336,128]{2,1,0:T(8,128)(2,1)S(1)} %copy-done, bf16[10,336,128]{2,1,0:T(8,128)(2,1)S(1)} %collective-permute-done.refs_1_, ...), custom_call_target="tpu_custom_call" | custom-call | tf_op jit(solution)/shard_map/pallas_call | solution.py:93
  69.2 0.0 copy-start.5
  69.2 0.0 copy-start.7
  69.3 18.6 %collective-permute-done.9.refs_11_ = bf16[15,336,128]{2,1,0:T(8,128)(2,1)S(1)} collective-permute-done((bf16[15,336,128]{2,1,0:T(8,128)(2,1)S(1)}, bf16[15,336,128]{2,1,0:T(8,128)(2,1)S(1)}, u32[]{:S(2)}, u32[]{:S(2)}) %collective-permute-start.9) | collective-permute-done | bytes 1290272 | tf_op jit(solution)/shard_map/ppermute | solution.py:27
  87.9 2.8 %collective-permute-done.8.refs_10_ = bf16[15,336,128]{2,1,0:T(8,128)(2,1)S(1)} collective-permute-done((bf16[15,336,128]{2,1,0:T(8,128)(2,1)S(1)}, bf16[15,336,128]{2,1,0:T(8,128)(2,1)S(1)}, u32[]{:S(2)}, u32[]{:S(2)}) %collective-permute-start.8) | collective-permute-done | bytes 1290272 | tf_op jit(solution)/shard_map/ppermute | solution.py:27
  90.7 0.0 collective-permute-done.7.refs_9_
  90.7 1.7 collective-permute-done.6.refs_8_
  92.4 1.5 collective-permute-start.11
  93.9 18.4 %collective-permute-start.10 = (bf16[20,336,128]{2,1,0:T(8,128)(2,1)S(1)}, bf16[20,336,128]{2,1,0:T(8,128)(2,1)S(1)}, u32[]{:S(2)}, u32[]{:S(2)}) collective-permute-start(bf16[20,336,128]{2,1,0:T(8,128)(2,1)S(1)} %get-tuple-element.43), channel_id=1, source_target_pairs={{0,16},{8,24},{16,0},{24,8},{32,48},{40,56},{48,32},{56,40},{64,80... | collective-permute-start | bytes 5160968 | tf_op jit(solution)/shard_map/ppermute | solution.py:27
  112.3 3.4 %shard_map.75 = (bf16[5,336,128]{2,1,0:T(8,128)(2,1)}, bf16[5,336,128]{2,1,0:T(8,128)(2,1)}, bf16[5,336,128]{2,1,0:T(8,128)(2,1)}, bf16[5,336,128]{2,1,0:T(8,128)(2,1)}) custom-call(s32[1]{0:T(128)} %bitcast.me_ref, s32[1280]{0:T(1024)S(1)} %reshape.53.table_ref, bf16[10,336,128]{2,1,0:T(8,128)(2,1)} %collective-permute-done.4.refs_0_.refs_2_, ...), custom_call_target="tpu_custom_call" | custom-call | tf_op jit(solution)/shard_map/pallas_call | solution.py:93
  115.7 13.4 %collective-permute-done.11.refs_17_ = bf16[20,336,128]{2,1,0:T(8,128)(2,1)S(1)} collective-permute-done((bf16[20,336,128]{2,1,0:T(8,128)(2,1)S(1)}, bf16[20,336,128]{2,1,0:T(8,128)(2,1)S(1)}, u32[]{:S(2)}, u32[]{:S(2)}) %collective-permute-start.11) | collective-permute-done | bytes 1720352 | tf_op jit(solution)/shard_map/ppermute | solution.py:27
  129.1 4.4 %collective-permute-done.10.refs_16_ = bf16[20,336,128]{2,1,0:T(8,128)(2,1)S(1)} collective-permute-done((bf16[20,336,128]{2,1,0:T(8,128)(2,1)S(1)}, bf16[20,336,128]{2,1,0:T(8,128)(2,1)S(1)}, u32[]{:S(2)}, u32[]{:S(2)}) %collective-permute-start.10) | collective-permute-done | bytes 1720352 | tf_op jit(solution)/shard_map/ppermute | solution.py:27
  133.6 1.2 copy-done.10
  134.8 0.8 collective-permute-start.14
  135.6 0.0 collective-permute-start.13
  135.6 2.0 %collective-permute-start.12 = (bf16[5,336,128]{2,1,0:T(8,128)(2,1)}, bf16[5,336,128]{2,1,0:T(8,128)(2,1)}, u32[]{:S(2)}, u32[]{:S(2)}) collective-permute-start(bf16[5,336,128]{2,1,0:T(8,128)(2,1)} %get-tuple-element.46), channel_id=1, source_target_pairs={{0,8},{8,16},{16,24},{24,0},{32,40},{40,48},{48,56},{56,32},{64,72... | collective-permute-start | bytes 1290248 | tf_op jit(solution)/shard_map/ppermute | solution.py:27
  137.6 1.7 copy.14
  139.3 1.4 reshape.55.cols_ref
  140.8 1.0 reshape.54.rank_ref
  141.8 0.7 dynamic_slice.3
  142.5 0.0 collective-permute-done.15.refs_15_
  142.5 2.3 %collective-permute-done.14.refs_14_ = bf16[5,336,128]{2,1,0:T(8,128)(2,1)S(1)} collective-permute-done((bf16[5,336,128]{2,1,0:T(8,128)(2,1)}, bf16[5,336,128]{2,1,0:T(8,128)(2,1)S(1)}, u32[]{:S(2)}, u32[]{:S(2)}) %collective-permute-start.14) | collective-permute-done | bytes 430112 | tf_op jit(solution)/shard_map/ppermute | solution.py:27
  144.8 0.0 collective-permute-done.13.refs_13_
  144.8 3.5 %collective-permute-done.12.refs_12_ = bf16[5,336,128]{2,1,0:T(8,128)(2,1)} collective-permute-done((bf16[5,336,128]{2,1,0:T(8,128)(2,1)}, bf16[5,336,128]{2,1,0:T(8,128)(2,1)}, u32[]{:S(2)}, u32[]{:S(2)}) %collective-permute-start.12) | collective-permute-done | bytes 430112 | tf_op jit(solution)/shard_map/ppermute | solution.py:27
  148.4 0.7 copy-done.6
  149.1 0.7 copy-done.8
  149.8 21.2 %shard_map.77 = bf16[1024,336]{1,0:T(8,128)(2,1)S(1)} custom-call(s32[1]{0:T(128)} %bitcast.me_ref, s32[1280]{0:T(1024)S(1)} %reshape.53.table_ref, s32[2560]{0:T(1024)S(1)} %reshape.54.rank_ref, s32[2560]{0:T(1024)S(1)} %copy-done.6, bf16[10,336,128]{2,1,0:T(8,128)(2,1)S(1)} %copy-done, bf16[10,336,128]{2,1,0:T(8,128)(2,1)S(1)} %collective-permute-done.refs_1_, ...), custom_call_target="tpu_custom_call" | custom-call | flops 7046430720 | bytes 37748736 | tf_op jit(solution)/shard_map/pallas_call | solution.py:208
  171.0 16.8 %all_to_all.5 = bf16[16,64,336]{2,1,0:T(8,128)(2,1)S(1)} all-to-all(bf16[16,64,336]{2,1,0:T(8,128)(2,1)S(1)} %bitcast.6), channel_id=1, replica_groups=mesh['site'=16,'scen'=8] {'site'}, dimensions={0} | all-to-all | bytes 1376256 | tf_op jit(solution)/shard_map/all_to_all | solution.py:267
  187.8 0.8 convert_reduce_fusion
  (31 shorter events, 0.1 us)
Async XLA Ops:
  6.5 34.0 %copy-start.17 = (s32[64,40]{0,1:T(8,128)S(1)}, s32[64,40]{0,1:T(8,128)}, u32[]{:S(2)}) copy-start(s32[64,40]{0,1:T(8,128)} %param.8) | copy-start | bytes 30724
  6.5 141.8 %all-gather.2.cloned.1.call-start = ((), (), s32[]{:S(2)}) async-start(), calls=%async_computation.1 | async-start | bytes 23592960 | tf_op jit(solution)/shard_map/all_gather | solution.py:226
  10.0 38.4 %copy-start = (bf16[10,336,128]{2,1,0:T(8,128)(2,1)S(1)}, bf16[10,336,128]{2,1,0:T(8,128)(2,1)}, u32[]{:S(2)}) copy-start(bf16[10,336,128]{2,1,0:T(8,128)(2,1)} %get-tuple-element.31.refs_0_) | copy-start | bytes 2580484
  10.0 21.5 %collective-permute-start = (bf16[10,336,128]{2,1,0:T(8,128)(2,1)}, bf16[10,336,128]{2,1,0:T(8,128)(2,1)S(1)}, u32[]{:S(2)}, u32[]{:S(2)}) collective-permute-start(bf16[10,336,128]{2,1,0:T(8,128)(2,1)} %get-tuple-element.31.refs_0_), channel_id=1, source_target_pairs={{0,96},{8,104},{16,112},{24,120},{32,0},{40,8},{48,16},{56,24},{64... | collective-permute-start | bytes 2580488 | tf_op jit(solution)/shard_map/ppermute | solution.py:27
  12.9 22.0 %collective-permute-start.1 = (bf16[10,336,128]{2,1,0:T(8,128)(2,1)}, bf16[10,336,128]{2,1,0:T(8,128)(2,1)S(1)}, u32[]{:S(2)}, u32[]{:S(2)}) collective-permute-start(bf16[10,336,128]{2,1,0:T(8,128)(2,1)} %get-tuple-element.31.refs_0_), channel_id=1, source_target_pairs={{0,32},{8,40},{16,48},{24,56},{32,64},{40,72},{48,80},{56,88},{64,... | collective-permute-start | bytes 2580488 | tf_op jit(solution)/shard_map/ppermute | solution.py:27
  12.9 22.0 %collective-permute-start.2 = (bf16[10,336,128]{2,1,0:T(8,128)(2,1)}, bf16[10,336,128]{2,1,0:T(8,128)(2,1)S(1)}, u32[]{:S(2)}, u32[]{:S(2)}) collective-permute-start(bf16[10,336,128]{2,1,0:T(8,128)(2,1)} %get-tuple-element.32.refs_3_.refs_4_), channel_id=1, source_target_pairs={{0,24},{8,0},{16,8},{24,16},{32,56},{40,32},{48,40},{56,48},{64,88... | collective-permute-start | bytes 2580488 | tf_op jit(solution)/shard_map/ppermute | solution.py:27
  15.9 21.7 %collective-permute-start.3 = (bf16[10,336,128]{2,1,0:T(8,128)(2,1)}, bf16[10,336,128]{2,1,0:T(8,128)(2,1)S(1)}, u32[]{:S(2)}, u32[]{:S(2)}) collective-permute-start(bf16[10,336,128]{2,1,0:T(8,128)(2,1)} %get-tuple-element.32.refs_3_.refs_4_), channel_id=1, source_target_pairs={{0,8},{8,16},{16,24},{24,0},{32,40},{40,48},{48,56},{56,32},{64,72... | collective-permute-start | bytes 2580488 | tf_op jit(solution)/shard_map/ppermute | solution.py:27
  34.9 29.5 %copy-start.2 = (bf16[10,336,128]{2,1,0:T(8,128)(2,1)}, bf16[10,336,128]{2,1,0:T(8,128)(2,1)S(1)}, u32[]{:S(2)}) copy-start(bf16[10,336,128]{2,1,0:T(8,128)(2,1)S(1)} %collective-permute-done.2.refs_4_.refs_5_) | copy-start | bytes 2580484
  37.6 0.9 copy-start.3
  38.5 21.2 %collective-permute-start.5 = (bf16[10,336,128]{2,1,0:T(8,128)(2,1)}, bf16[10,336,128]{2,1,0:T(8,128)(2,1)}, u32[]{:S(2)}, u32[]{:S(2)}) collective-permute-start(bf16[10,336,128]{2,1,0:T(8,128)(2,1)} %get-tuple-element.32.refs_3_.refs_4_), channel_id=1, source_target_pairs={{0,16},{8,24},{16,0},{24,8},{32,48},{40,56},{48,32},{56,40},{64,80... | collective-permute-start | bytes 2580488 | tf_op jit(solution)/shard_map/ppermute | solution.py:27
  39.0 21.2 %collective-permute-start.4 = (bf16[10,336,128]{2,1,0:T(8,128)(2,1)}, bf16[10,336,128]{2,1,0:T(8,128)(2,1)}, u32[]{:S(2)}, u32[]{:S(2)}) collective-permute-start(bf16[10,336,128]{2,1,0:T(8,128)(2,1)} %get-tuple-element.31.refs_0_), channel_id=1, source_target_pairs={{0,64},{8,72},{16,80},{24,88},{32,96},{40,104},{48,112},{56,120},{... | collective-permute-start | bytes 2580488 | tf_op jit(solution)/shard_map/ppermute | solution.py:27
  40.6 0.6 copy-start.16
  45.7 0.6 copy-start.15
  48.4 1.3 copy-start.1
  49.7 1.2 copy-start.4
  60.2 27.7 %collective-permute-start.9 = (bf16[15,336,128]{2,1,0:T(8,128)(2,1)S(1)}, bf16[15,336,128]{2,1,0:T(8,128)(2,1)S(1)}, u32[]{:S(2)}, u32[]{:S(2)}) collective-permute-start(bf16[15,336,128]{2,1,0:T(8,128)(2,1)S(1)} %get-tuple-element.40), channel_id=1, source_target_pairs={{0,96},{8,104},{16,112},{24,120},{32,0},{40,8},{48,16},{56,24},{64... | collective-permute-start | bytes 3870728 | tf_op jit(solution)/shard_map/ppermute | solution.py:27
  62.4 28.3 %collective-permute-start.8 = (bf16[15,336,128]{2,1,0:T(8,128)(2,1)S(1)}, bf16[15,336,128]{2,1,0:T(8,128)(2,1)S(1)}, u32[]{:S(2)}, u32[]{:S(2)}) collective-permute-start(bf16[15,336,128]{2,1,0:T(8,128)(2,1)S(1)} %get-tuple-element.38), channel_id=1, source_target_pairs={{0,32},{8,40},{16,48},{24,56},{32,64},{40,72},{48,80},{56,88},{64,... | collective-permute-start | bytes 3870728 | tf_op jit(solution)/shard_map/ppermute | solution.py:27
  62.4 28.3 %collective-permute-start.7 = (bf16[15,336,128]{2,1,0:T(8,128)(2,1)S(1)}, bf16[15,336,128]{2,1,0:T(8,128)(2,1)S(1)}, u32[]{:S(2)}, u32[]{:S(2)}) collective-permute-start(bf16[15,336,128]{2,1,0:T(8,128)(2,1)S(1)} %get-tuple-element.36), channel_id=1, source_target_pairs={{0,24},{8,0},{16,8},{24,16},{32,56},{40,32},{48,40},{56,48},{64,88... | collective-permute-start | bytes 3870728 | tf_op jit(solution)/shard_map/ppermute | solution.py:27
  64.3 28.1 %collective-permute-start.6 = (bf16[15,336,128]{2,1,0:T(8,128)(2,1)S(1)}, bf16[15,336,128]{2,1,0:T(8,128)(2,1)S(1)}, u32[]{:S(2)}, u32[]{:S(2)}) collective-permute-start(bf16[15,336,128]{2,1,0:T(8,128)(2,1)S(1)} %get-tuple-element.34), channel_id=1, source_target_pairs={{0,8},{8,16},{16,24},{24,0},{32,40},{40,48},{48,56},{56,32},{64,72... | collective-permute-start | bytes 3870728 | tf_op jit(solution)/shard_map/ppermute | solution.py:27
  69.2 79.1 %copy-start.5 = (bf16[168,168]{1,0:T(8,128)(2,1)S(1)}, bf16[168,168]{1,0:T(8,128)(2,1)}, u32[]{:S(2)}) copy-start(bf16[168,168]{1,0:T(8,128)(2,1)} %refs_19_.1) | copy-start | bytes 169348
  69.2 79.1 %copy-start.7 = (f32[1024]{0:T(1024)S(1)}, f32[1024]{0:T(1024)}, u32[]{:S(2)}) copy-start(f32[1024]{0:T(1024)} %param.11) | copy-start | bytes 12292
  87.9 47.7 %copy-start.11 = (bf16[15,336,128]{2,1,0:T(8,128)(2,1)}, bf16[15,336,128]{2,1,0:T(8,128)(2,1)S(1)}, u32[]{:S(2)}) copy-start(bf16[15,336,128]{2,1,0:T(8,128)(2,1)S(1)} %collective-permute-done.9.refs_11_) | copy-start | bytes 3870724
  90.7 44.9 %copy-start.12 = (bf16[15,336,128]{2,1,0:T(8,128)(2,1)}, bf16[15,336,128]{2,1,0:T(8,128)(2,1)S(1)}, u32[]{:S(2)}) copy-start(bf16[15,336,128]{2,1,0:T(8,128)(2,1)S(1)} %collective-permute-done.8.refs_10_) | copy-start | bytes 3870724
  90.7 44.9 %copy-start.13 = (bf16[15,336,128]{2,1,0:T(8,128)(2,1)}, bf16[15,336,128]{2,1,0:T(8,128)(2,1)S(1)}, u32[]{:S(2)}) copy-start(bf16[15,336,128]{2,1,0:T(8,128)(2,1)S(1)} %collective-permute-done.7.refs_9_) | copy-start | bytes 3870724
  92.4 43.2 %copy-start.14 = (bf16[15,336,128]{2,1,0:T(8,128)(2,1)}, bf16[15,336,128]{2,1,0:T(8,128)(2,1)S(1)}, u32[]{:S(2)}) copy-start(bf16[15,336,128]{2,1,0:T(8,128)(2,1)S(1)} %collective-permute-done.6.refs_8_) | copy-start | bytes 3870724
  92.4 36.7 %collective-permute-start.11 = (bf16[20,336,128]{2,1,0:T(8,128)(2,1)S(1)}, bf16[20,336,128]{2,1,0:T(8,128)(2,1)S(1)}, u32[]{:S(2)}, u32[]{:S(2)}) collective-permute-start(bf16[20,336,128]{2,1,0:T(8,128)(2,1)S(1)} %get-tuple-element.45), channel_id=1, source_target_pairs={{0,64},{8,72},{16,80},{24,88},{32,96},{40,104},{48,112},{56,120},{... | collective-permute-start | bytes 5160968 | tf_op jit(solution)/shard_map/ppermute | solution.py:27
  93.9 39.7 %collective-permute-start.10 = (bf16[20,336,128]{2,1,0:T(8,128)(2,1)S(1)}, bf16[20,336,128]{2,1,0:T(8,128)(2,1)S(1)}, u32[]{:S(2)}, u32[]{:S(2)}) collective-permute-start(bf16[20,336,128]{2,1,0:T(8,128)(2,1)S(1)} %get-tuple-element.43), channel_id=1, source_target_pairs={{0,16},{8,24},{16,0},{24,8},{32,48},{40,56},{48,32},{56,40},{64,80... | collective-permute-start | bytes 5160968 | tf_op jit(solution)/shard_map/ppermute | solution.py:27
  129.1 4.4 %copy-start.9 = (bf16[20,336,128]{2,1,0:T(8,128)(2,1)}, bf16[20,336,128]{2,1,0:T(8,128)(2,1)S(1)}, u32[]{:S(2)}) copy-start(bf16[20,336,128]{2,1,0:T(8,128)(2,1)S(1)} %collective-permute-done.11.refs_17_) | copy-start | bytes 5160964
  133.6 1.2 copy-start.10
  133.6 9.0 %collective-permute-start.15 = (bf16[5,336,128]{2,1,0:T(8,128)(2,1)}, bf16[5,336,128]{2,1,0:T(8,128)(2,1)S(1)}, u32[]{:S(2)}, u32[]{:S(2)}) collective-permute-start(bf16[5,336,128]{2,1,0:T(8,128)(2,1)} %get-tuple-element.52), channel_id=1, source_target_pairs={{0,96},{8,104},{16,112},{24,120},{32,0},{40,8},{48,16},{56,24},{64... | collective-permute-start | bytes 1290248 | tf_op jit(solution)/shard_map/ppermute | solution.py:27
  134.8 10.0 %collective-permute-start.14 = (bf16[5,336,128]{2,1,0:T(8,128)(2,1)}, bf16[5,336,128]{2,1,0:T(8,128)(2,1)S(1)}, u32[]{:S(2)}, u32[]{:S(2)}) collective-permute-start(bf16[5,336,128]{2,1,0:T(8,128)(2,1)} %get-tuple-element.50), channel_id=1, source_target_pairs={{0,32},{8,40},{16,48},{24,56},{32,64},{40,72},{48,80},{56,88},{64,... | collective-permute-start | bytes 1290248 | tf_op jit(solution)/shard_map/ppermute | solution.py:27
  135.6 9.2 %collective-permute-start.13 = (bf16[5,336,128]{2,1,0:T(8,128)(2,1)}, bf16[5,336,128]{2,1,0:T(8,128)(2,1)}, u32[]{:S(2)}, u32[]{:S(2)}) collective-permute-start(bf16[5,336,128]{2,1,0:T(8,128)(2,1)} %get-tuple-element.48), channel_id=1, source_target_pairs={{0,24},{8,0},{16,8},{24,16},{32,56},{40,32},{48,40},{56,48},{64,88... | collective-permute-start | bytes 1290248 | tf_op jit(solution)/shard_map/ppermute | solution.py:27
  135.6 12.7 %collective-permute-start.12 = (bf16[5,336,128]{2,1,0:T(8,128)(2,1)}, bf16[5,336,128]{2,1,0:T(8,128)(2,1)}, u32[]{:S(2)}, u32[]{:S(2)}) collective-permute-start(bf16[5,336,128]{2,1,0:T(8,128)(2,1)} %get-tuple-element.46), channel_id=1, source_target_pairs={{0,8},{8,16},{16,24},{24,0},{32,40},{40,48},{48,56},{56,32},{64,72... | collective-permute-start | bytes 1290248 | tf_op jit(solution)/shard_map/ppermute | solution.py:27
  148.4 0.7 copy-start.6
  149.1 0.7 copy-start.8
Sparse Core Ops, SparseCore 0:
  9.1 103.8 all-gather.1

commit v3 on v2

v3 whole, which is shorter than its diff:
```python
import functools

import jax
import jax.numpy as jnp
from jax import lax
from jax.experimental import pallas as pl
from jax.experimental.pallas import tpu as pltpu
from jax.sharding import PartitionSpec as P

BLK = 256
HALF = 128
HOURS = 168
NZ = 40
SLOTS = 5
FEW = 5
RB_DEV = 4
CB_DEV = 10
SIDE = 4
BUSES = 1024
COLS = 160
ALL_VMEM = 60 << 20


def shift(value, dx, dy):
    n = SIDE
    pairs = [
        (x * n + y, ((x + dx) % n) * n + (y + dy) % n) for x in range(n) for y in range(n)
    ]
    return lax.ppermute(value, "site", pairs)


def step(value, axis, d):
    return shift(value, d, 0) if axis == 0 else shift(value, 0, d)


def after(value, *others):
    return lax.optimization_barrier((value, *others))[0]


VMEM = pl.BlockSpec(memory_space=pltpu.VMEM)


def reblock_kernel(z_ref, *outs):
    for b in range(CB_DEV):
        for h in range(2):
            start = b * BLK + h * HALF
            outs[h * 2 + b // FEW][b % FEW] = z_ref[:, start : start + HALF]


def reblocked(normals_t):
    width = normals_t.shape[0]
    out = jax.ShapeDtypeStruct((FEW, width, HALF), normals_t.dtype)
    return pl.pallas_call(
        reblock_kernel,
        in_specs=[VMEM],
        out_specs=[VMEM] * 4,
        out_shape=[out] * 4,
        compiler_params=pltpu.CompilerParams(vmem_limit_bytes=ALL_VMEM),
    )(normals_t)


ANY = pl.BlockSpec(memory_space=pl.ANY)


def start_block(pair, local, target, sem):
    @pl.when(local < FEW)
    def _():
        pltpu.make_async_copy(pair[0].at[jnp.minimum(local, FEW - 1)], target, sem).start()

    @pl.when(local >= FEW)
    def _():
        pltpu.make_async_copy(pair[1].at[jnp.maximum(local - FEW, 0)], target, sem).start()


def wait_block(pair, target, sem):
    pltpu.make_async_copy(pair[0].at[0], target, sem).wait()


def pairs(refs):
    return [refs[k : k + 2] for k in range(0, len(refs), 2)]


def device_at(x, y, ex, ey):
    return lax.rem(x + ex, SIDE) * SIDE + lax.rem(y + ey, SIDE)


def pick_kernel(hops, holders, aliased, me_ref, table_ref, *refs):
    span, count = len(holders), 2 * len(hops)
    held = pairs(refs[: 4 * span])
    refs = refs[4 * span + aliased * count :]
    outs, buffers, came, gone = refs[:count], *refs[count:]
    x, y = me_ref[0] // SIDE, lax.rem(me_ref[0], SIDE)
    for k in range(count):
        axis, d = k // len(hops), hops[k % len(hops)]
        user = device_at(x, y, 0, d) if axis == 0 else device_at(x, y, d, 0)
        for i, e in enumerate(holders):
            holder = device_at(x, y, e, 0) if axis == 0 else device_at(x, y, 0, e)
            for s in range(SLOTS):
                local = table_ref[(user * SIDE * SIDE + holder) * SLOTS + s]
                start_block(held[axis * span + i], local, buffers.at[k, i, s], came.at[k])
    for k in range(count):
        for i in range(span):
            pltpu.make_async_copy(held[0][0], buffers.at[k, i], came.at[k]).wait()
        for i, e in enumerate(holders):
            target = outs[k].at[pl.ds(e * SLOTS, SLOTS)]
            pltpu.make_async_copy(buffers.at[k, i], target, gone.at[k, i]).start()
    for k in range(count):
        for i, e in enumerate(holders):
            target = outs[k].at[pl.ds(e * SLOTS, SLOTS)]
            pltpu.make_async_copy(buffers.at[k, i], target, gone.at[k, i]).wait()


def picked(hops, holders, scalars, lines, begun=()):
    width = lines[0][0][0].shape[1]
    out = jax.ShapeDtypeStruct((SIDE * SLOTS, width, HALF), jnp.bfloat16)
    outs, span = 2 * len(hops), len(holders)
    held = [p for line in lines for e in holders for p in line[e]]
    return pl.pallas_call(
        functools.partial(pick_kernel, hops, holders, bool(begun)),
        grid_spec=pltpu.PrefetchScalarGridSpec(
            num_scalar_prefetch=2,
            grid=(),
            in_specs=[ANY] * (len(held) + len(begun)),
            out_specs=[ANY] * outs,
            scratch_shapes=[
                pltpu.VMEM((outs, span, SLOTS, width, HALF), out.dtype),
                pltpu.SemaphoreType.DMA((outs,)),
                pltpu.SemaphoreType.DMA((outs, span)),
            ],
        ),
        out_shape=[out] * outs,
        input_output_aliases={2 + len(held) + k: k for k in range(len(begun))},
        compiler_params=pltpu.CompilerParams(vmem_limit_bytes=ALL_VMEM),
    )(*scalars, *held, *begun)


def slots_of(ex, ey):
    return (ex * SIDE + ey) * SLOTS


NT = (((1,), (1,)), ((), ()))


def early_kernel(me_ref, table_ref, rank_ref, cols_ref, *refs):
    held, sent, f_ref, bus_ref, acc_ref, use_ref, onehot_ref, zlo, zhi, sem = (
        pairs(refs[:16]), refs[16:20], *refs[20:]
    )
    r = pl.program_id(0)
    me = me_ref[0]
    x, y = me // SIDE, lax.rem(me, SIDE)

    def slot_at(t):
        col = cols_ref[(me * RB_DEV + r) * NZ + t]
        holder = col // CB_DEV
        ex = lax.rem(holder // SIDE - x + SIDE, SIDE)
        ey = lax.rem(lax.rem(holder, SIDE) - y + SIDE, SIDE)
        return slots_of(ex, ey) + rank_ref[me * COLS + col]

    @pl.when(r == 0)
    def _():
        for axis, z in ((0, zlo), (1, zhi)):
            for e in range(SIDE):
                for d in range(SIDE):
                    ex, ey = (e, d) if axis == 0 else (d, e)
                    base = slots_of(ex, ey)
                    if d == 2:
                        z[base : base + SLOTS] = jnp.zeros((SLOTS, *z.shape[1:]), z.dtype)
                    elif d:
                        source = sent[axis * 2 + (3 - d) // 2].at[pl.ds(e * SLOTS, SLOTS)]
                        pltpu.make_async_copy(source, z.at[pl.ds(base, SLOTS)], sem).start()
                    else:
                        holder = device_at(x, y, ex, ey)
                        for s in range(SLOTS):
                            local = table_ref[(me * SIDE * SIDE + holder) * SLOTS + s]
                            start_block(held[axis * SIDE + e], local, z.at[base + s], sem)
        for z in (zlo, zhi):
            for k in range(SIDE * (SIDE - 1)):
                part = z.at[pl.ds(k * SLOTS, SLOTS)]
                pltpu.make_async_copy(held[0][0], part, sem).wait()

    @pl.loop(0, SIDE * SIDE * SLOTS)
    def _(k):
        use_ref[r * SIDE * SIDE * SLOTS + k] = -1

    total = None
    for t in range(NZ):
        slot = slot_at(t)
        use_ref[r * SIDE * SIDE * SLOTS + slot] = t
        z = jnp.concatenate([zlo[slot], zhi[slot]], axis=1)
        term = lax.dot_general(z, f_ref[0, t], NT, preferred_element_type=jnp.float32)
        total = term if total is None else total + term
    acc_ref[0] = total
    buses = lax.broadcasted_iota(jnp.int32, (BUSES, BLK), 0)
    onehot_ref[...] = jnp.where(buses == bus_ref[0], 1.0, 0.0).astype(jnp.bfloat16)


def early(scalars, arrays, factor, bus):
    width = arrays[0].shape[1]
    slots = SIDE * SIDE * SLOTS
    grid_spec = pltpu.PrefetchScalarGridSpec(
        num_scalar_prefetch=len(scalars),
        grid=(RB_DEV,),
        in_specs=[ANY] * len(arrays)
        + [
            pl.BlockSpec((1, NZ, BLK, BLK), lambda r, *_: (r, 0, 0, 0)),
            pl.BlockSpec((1, 1, BLK), lambda r, *_: (r, 0, 0)),
        ],
        out_specs=[
            pl.BlockSpec((1, width, BLK), lambda r, *_: (r, 0, 0)),
            pl.BlockSpec(memory_space=pltpu.SMEM),
            pl.BlockSpec((BUSES, BLK), lambda r, *_: (0, r)),
        ],
        scratch_shapes=[
            pltpu.VMEM((slots, width, HALF), jnp.bfloat16),
            pltpu.VMEM((slots, width, HALF), jnp.bfloat16),
            pltpu.SemaphoreType.DMA,
        ],
    )
    return pl.pallas_call(
        early_kernel,
        grid_spec=grid_spec,
        out_shape=[
            jax.ShapeDtypeStruct((RB_DEV, width, BLK), jnp.float32),
            jax.ShapeDtypeStruct((RB_DEV * slots,), jnp.int32),
            jax.ShapeDtypeStruct((BUSES, RB_DEV * BLK), jnp.bfloat16),
        ],
        compiler_params=pltpu.CompilerParams(vmem_limit_bytes=ALL_VMEM),
        cost_estimate=pl.CostEstimate(
            flops=2 * RB_DEV * NZ * BLK * BLK * width, bytes_accessed=36 << 20, transcendentals=0
        ),
    )(*scalars, *arrays, factor, bus)


def late_kernel(use_ref, lo_ref, hi_ref, f_ref, acc_ref, temporal_ref, cap_ref, spr_ref, onehot_ref, *refs):
    out_ref, onehot, injected, sem = refs
    r = pl.program_id(0)
    base = r * SIDE * SIDE * SLOTS

    @pl.when(r == 0)
    def _():
        pltpu.make_async_copy(onehot_ref, onehot, sem).start()

    def piece(slot, half):
        t = use_ref[base + slot]
        f = f_ref[0, jnp.maximum(t, 0), :, half * HALF : (half + 1) * HALF]
        return jnp.where(t >= 0, f, jnp.zeros_like(f))

    total = acc_ref[0]
    for e in range(SIDE):
        for s in range(SLOTS):
            z = jnp.concatenate([lo_ref[e * SLOTS + s], hi_ref[e * SLOTS + s]], axis=1)
            f = jnp.concatenate(
                [piece(slots_of(e, 2) + s, 0), piece(slots_of(2, e) + s, 1)], axis=1
            )
            total += lax.dot_general(z, f, NT, preferred_element_type=jnp.float32)
    cap, spr = cap_ref[0], spr_ref[0]
    parts = []
    for s in range(total.shape[0] // HOURS):
        spatial = total[s * HOURS : (s + 1) * HOURS].astype(jnp.bfloat16)
        weather = jnp.dot(temporal_ref[...], spatial, preferred_element_type=jnp.float32)
        parts.append(cap * jnp.exp(spr * weather - 0.5 * spr * spr))
    injected[r] = jnp.concatenate(parts, axis=0).astype(jnp.bfloat16)

    @pl.when(r == pl.num_programs(0) - 1)
    def _():
        pltpu.make_async_copy(onehot_ref, onehot, sem).wait()
        rows = jnp.concatenate([injected[k] for k in range(RB_DEV)], axis=1)
        power = lax.dot_general(onehot[...], rows, NT, preferred_element_type=jnp.float32)
        out_ref[...] = power.astype(jnp.bfloat16)


def late(use, opposite, factor, acc, temporal, vectors, onehot):
    width = acc.shape[1]
    vec = pl.BlockSpec((1, 1, BLK), lambda r, *_: (r, 0, 0))
    grid_spec = pltpu.PrefetchScalarGridSpec(
        num_scalar_prefetch=1,
        grid=(RB_DEV,),
        in_specs=[
            pl.BlockSpec(opposite[0].shape, lambda r, *_: (0, 0, 0)),
            pl.BlockSpec(opposite[0].shape, lambda r, *_: (0, 0, 0)),
            pl.BlockSpec((1, NZ, BLK, BLK), lambda r, *_: (r, 0, 0, 0)),
            pl.BlockSpec((1, width, BLK), lambda r, *_: (r, 0, 0)),
            pl.BlockSpec((HOURS, HOURS), lambda r, *_: (0, 0)),
            vec,
            vec,
            ANY,
        ],
        out_specs=pl.BlockSpec((BUSES, width), lambda r, *_: (0, 0)),
        scratch_shapes=[
            pltpu.VMEM(onehot.shape, onehot.dtype),
            pltpu.VMEM((RB_DEV, width, BLK), jnp.bfloat16),
            pltpu.SemaphoreType.DMA,
        ],
    )
    return pl.pallas_call(
        late_kernel,
        grid_spec=grid_spec,
        out_shape=jax.ShapeDtypeStruct((BUSES, width), jnp.bfloat16),
        compiler_params=pltpu.CompilerParams(vmem_limit_bytes=ALL_VMEM),
        cost_estimate=pl.CostEstimate(
            flops=RB_DEV * NZ * BLK * BLK * width,
            bytes_accessed=28 << 20,
            transcendentals=RB_DEV * BLK * width,
        ),
    )(use, *opposite, factor, acc, temporal, *vectors, onehot)


def shards(normals, pattern, factor, temporal, capacity, spread, bus_map):
    n = SIDE
    sites = n * n
    me = lax.axis_index("site")
    portion = lax.all_gather(factor, "scen", axis=2, tiled=True)

    ids = jnp.arange(sites * CB_DEV, dtype=jnp.int32)
    wanted = pattern.reshape(sites, -1)
    needed = jnp.any(wanted[:, :, None] == ids[None, None, :], axis=1)
    needed = needed.reshape(sites, sites, CB_DEV).astype(jnp.int32)
    lower = (jnp.arange(CB_DEV)[:, None] < jnp.arange(CB_DEV)[None, :]).astype(jnp.int32)
    rank = jnp.sum(needed[:, :, :, None] * lower[None, None], axis=2)
    slot_ids = jnp.arange(SLOTS, dtype=jnp.int32)
    chosen = (needed[..., None] == 1) & (rank[..., None] == slot_ids)
    local_ids = jnp.arange(CB_DEV, dtype=jnp.int32)
    table = jnp.sum(jnp.where(chosen, local_ids[:, None], 0), axis=2)

    table = table.reshape(-1)
    index = me.reshape(1).astype(jnp.int32)

    parts = reblocked(normals.T)
    lines = [[tuple(parts[2 * axis : 2 * axis + 2]), None, None, None] for axis in (0, 1)]
    ring = [(axis, e) for axis in (0, 1) for e in (1, 3)]
    below = [step(lines[axis][0][0], axis, 1) for axis in (0, 1)]
    above = [step(lines[axis][0][1], axis, -1) for axis in (0, 1)]
    first = below + above
    for axis in (0, 1):
        own = lines[axis][0]
        lines[axis][3] = (below[axis], step(after(own[1], *first), axis, 1))
        lines[axis][1] = (step(after(own[0], *first), axis, -1), above[axis])
    for axis in (0, 1):
        lines[axis][2] = (step(after(below[axis], table), axis, 1), step(above[axis], axis, -1))
    tables = (index, table)
    out = picked((1, 3), (0, 1, 3), tables, lines)
    out = picked((1, 3), (2,), tables, lines, out)
    sent = [step(b, 1 - axis, d) for b, (axis, d) in zip(out, ring)]
    flat = (rank.reshape(-1), pattern.reshape(-1))
    held = RB_DEV * BLK
    bus = lax.dynamic_slice_in_dim(bus_map, me * held, held, 0)
    out = picked((2,), (0, 1, 2, 3), (after(index, out[0], *flat, bus), table), lines)
    opposite = [step(after(b, *sent), 1 - axis, 2) for axis, b in enumerate(out)]
    arrays = [p for line in lines for pair in line for p in pair] + sent
    shape = (RB_DEV, 1, BLK)
    scalars = (index, table, *flat)
    vectors = (capacity.reshape(shape), spread.reshape(shape))
    acc, use, onehot = early(scalars, arrays, portion, bus.reshape(shape))
    power = late(use, opposite, portion, acc, temporal, vectors, onehot)
    tiles = lax.all_to_all(power.reshape(sites, -1, power.shape[1]), "site", 0, 0, tiled=True)
    return jnp.sum(tiles.astype(jnp.float32), axis=0)


def solution(mesh):
    placed = (P("site", "scen"), P(), P("site", None, "scen", None), P(), P("site"), P("site"), P())
    return jax.shard_map(
        shards, mesh=mesh, in_specs=placed, out_specs=P("site", "scen"), check_vma=False
    )
```

time: 197 us -> 181 us (0.919)
  waiting for transfers between devices: 70.1 us -> 57.7 us
  Pallas kernels: 40.7 us -> 50.1 us
  local copies, waits for them, and re-layouts: 16.3 us -> 9.97 us
  starting transfers between devices: 34.8 us -> 28.5 us
    ppermute x16 -> x18, waiting for transfers between devices: 69.4 us -> 57 us  [shift(): return lax.ppermute(value, 'site', pairs)]
    pallas_call x5 -> x6, Pallas kernels: 40.7 us -> 50.1 us  [the longest x1 20.5 us: early(): pl.pallas_call(early_kernel, grid_spec=grid_spec, out_shape=[jax.ShapeDty...]
    ppermute x16 -> x18, starting transfers between devices: 34.8 us -> 28.5 us  [shift(): return lax.ppermute(value, 'site', pairs)]
    unnamed x37 -> x27, local copies, waits for them, and re-layouts: 6.66 us -> 4.06 us
  transfers between devices with their start and end apart: 17 -> 19, of which waited for: 12 -> 8; matrix products, arithmetic and copies ran while one was open for 6% -> 4% of each run, Pallas kernels for 10% -> 20%
where the time goes in v3:
time: 181 us; the launch traced here: 180 us
  waiting for transfers between devices  57.7 us (32%)
  Pallas kernels  50.1 us (28%)
  starting transfers between devices  28.5 us (16%)
  blocking collectives  18.1 us (10%)
  between operations  13.6 us (8%)
  local copies, waits for them, and re-layouts  9.97 us (6%)
    ppermute x18, waiting for transfers between devices, shift(): return lax.ppermute(value, 'site', pairs)  57 us
    ppermute x18, starting transfers between devices, shift(): return lax.ppermute(value, 'site', pairs)  28.5 us
    pallas_call x1, Pallas kernels, early(): pl.pallas_call(early_kernel, grid_spec=grid_spec, out_shape=[jax.ShapeDty...  20.5 us
    all_to_all x1, blocking collectives, shards(): lax.all_to_all(power.reshape(sites, -1, power.shape[1]), 'site', 0, 0, ti...  18.1 us
    pallas_call x1, Pallas kernels, late(): pl.pallas_call(late_kernel, grid_spec=grid_spec, out_shape=jax.ShapeDtype...  13.8 us
    pallas_call x3, Pallas kernels, picked(): pl.pallas_call(functools.partial(pick_kernel, hops, holders, bool(begun))...  12.8 us
    unnamed x27, local copies, waits for them, and re-layouts  4.06 us
  transfers between devices with their start and end apart: 19, of which 8 were waited for; matrix products, arithmetic and copies ran while one was open for 4% of the time, Pallas kernels for 20%

profile of v3, /device:TPU:64, one launch (start us, length us, event | category | flops | bytes accessed | tf_op | source)
XLA Modules:
  0.0 179.6 jit_solution(16954771996023914085)
XLA Ops:
  6.5 0.7 all-gather.2.cloned.1.call-update
  7.3 3.0 %shard_map.73 = (bf16[5,336,128]{2,1,0:T(8,128)(2,1)}, bf16[5,336,128]{2,1,0:T(8,128)(2,1)}, bf16[5,336,128]{2,1,0:T(8,128)(2,1)}, bf16[5,336,128]{2,1,0:T(8,128)(2,1)}) custom-call(bf16[336,2560]{1,0:T(8,128)(2,1)} %bitcast.7), custom_call_target="tpu_custom_call" | custom-call | tf_op jit(solution)/shard_map/pallas_call | solution.py:53
  10.2 1.5 collective-permute-start
  11.7 1.6 collective-permute-start.1
  13.3 1.7 collective-permute-start.2
  15.1 1.7 collective-permute-start.3
  16.7 0.1 copy.14
  16.8 0.1 eq.39
  16.9 0.5 fusion
  17.4 0.1 reshape.60
  17.5 5.8 %collective-permute-done.refs_4_.refs_6_ = bf16[5,336,128]{2,1,0:T(8,128)(2,1)S(1)} collective-permute-done((bf16[5,336,128]{2,1,0:T(8,128)(2,1)}, bf16[5,336,128]{2,1,0:T(8,128)(2,1)S(1)}, u32[]{:S(2)}, u32[]{:S(2)}) %collective-permute-start) | collective-permute-done | bytes 430112 | tf_op jit(solution)/shard_map/ppermute | solution.py:29
  23.3 1.3 collective-permute-done.1.refs_10_.refs_14_
  24.6 0.0 collective-permute-done.2.refs_3_
  24.6 1.5 collective-permute-done.3.refs_9_.refs_11_
  26.1 1.6 collective-permute-start.4
  27.6 0.5 collective-permute-start.7
  28.1 2.9 %collective-permute-start.8 = (bf16[5,336,128]{2,1,0:T(8,128)(2,1)}, bf16[5,336,128]{2,1,0:T(8,128)(2,1)}, u32[]{:S(2)}, u32[]{:S(2)}) collective-permute-start(bf16[5,336,128]{2,1,0:T(8,128)(2,1)} %get-tuple-element.38.refs_6_.refs_8_), channel_id=1, source_target_pairs={{0,24},{8,0},{16,8},{24,16},{32,56},{40,32},{48,40},{56,48},{64,88... | collective-permute-start | bytes 1290248 | tf_op jit(solution)/shard_map/ppermute | solution.py:29
  31.1 0.2 copy.16
  31.2 0.2 copy.15
  31.4 0.2 multiply_reduce_fusion
  31.6 0.1 select_reduce_fusion
  31.7 0.2 copy.17
  31.9 0.8 reshape.53.table_ref
  32.7 0.3 collective-permute-start.5
  32.9 0.0 collective-permute-start.11
  33.0 3.3 %collective-permute-done.4.refs_2_ = bf16[5,336,128]{2,1,0:T(8,128)(2,1)} collective-permute-done((bf16[5,336,128]{2,1,0:T(8,128)(2,1)}, bf16[5,336,128]{2,1,0:T(8,128)(2,1)}, u32[]{:S(2)}, u32[]{:S(2)}) %collective-permute-start.4) | collective-permute-done | bytes 430112 | tf_op jit(solution)/shard_map/ppermute | solution.py:29
  36.3 1.6 collective-permute-start.9
  37.8 4.2 %collective-permute-done.7.refs_5_.refs_7_ = bf16[5,336,128]{2,1,0:T(8,128)(2,1)} collective-permute-done((bf16[5,336,128]{2,1,0:T(8,128)(2,1)}, bf16[5,336,128]{2,1,0:T(8,128)(2,1)}, u32[]{:S(2)}, u32[]{:S(2)}) %collective-permute-start.7) | collective-permute-done | bytes 430112 | tf_op jit(solution)/shard_map/ppermute | solution.py:29
  42.0 0.0 collective-permute-start.6
  42.0 0.0 collective-permute-done.8.refs_8_.refs_10_
  42.0 2.9 %collective-permute-start.10 = (bf16[5,336,128]{2,1,0:T(8,128)(2,1)S(1)}, bf16[5,336,128]{2,1,0:T(8,128)(2,1)S(1)}, u32[]{:S(2)}, u32[]{:S(2)}) collective-permute-start(bf16[5,336,128]{2,1,0:T(8,128)(2,1)S(1)} %collective-permute-done.3.refs_9_.refs_11_), channel_id=1, source_target_pairs={{0,24},{8,0},{16,8},{24,16},{32,56},{40,32},{48,40},{56,48},{64,88... | collective-permute-start | bytes 1290248 | tf_op jit(solution)/shard_map/ppermute | solution.py:29
  44.9 2.4 %collective-permute-done.11.refs_11_.refs_15_ = bf16[5,336,128]{2,1,0:T(8,128)(2,1)} collective-permute-done((bf16[5,336,128]{2,1,0:T(8,128)(2,1)}, bf16[5,336,128]{2,1,0:T(8,128)(2,1)}, u32[]{:S(2)}, u32[]{:S(2)}) %collective-permute-start.11) | collective-permute-done | bytes 430112 | tf_op jit(solution)/shard_map/ppermute | solution.py:29
  47.3 5.3 %shard_map.74 = (bf16[20,336,128]{2,1,0:T(8,128)(2,1)}, bf16[20,336,128]{2,1,0:T(8,128)(2,1)}, bf16[20,336,128]{2,1,0:T(8,128)(2,1)}, bf16[20,336,128]{2,1,0:T(8,128)(2,1)}) custom-call(s32[1]{0:T(128)} %bitcast.me_ref, s32[1280]{0:T(1024)} %reshape.53.table_ref, bf16[5,336,128]{2,1,0:T(8,128)(2,1)} %get-tuple-element.35.refs_0_, ...), custom_call_target="tpu_custom_call" | custom-call | tf_op jit(solution)/shard_map/pallas_call | solution.py:118
  52.6 0.0 collective-permute-done.5.refs_0_.refs_4_
  52.6 0.0 collective-permute-done.6.refs_1_.refs_5_
  52.7 0.0 collective-permute-done.10.refs_3_.refs_13_
  52.7 0.7 copy-done
  53.4 0.2 copy-done.2
  53.6 0.1 copy-done.1
  53.7 0.2 copy-done.3
  53.8 3.2 %shard_map.75 = (bf16[20,336,128]{2,1,0:T(8,128)(2,1)}, bf16[20,336,128]{2,1,0:T(8,128)(2,1)}, bf16[20,336,128]{2,1,0:T(8,128)(2,1)}, bf16[20,336,128]{2,1,0:T(8,128)(2,1)}) custom-call(s32[1]{0:T(128)} %bitcast.me_ref, s32[1280]{0:T(1024)} %reshape.53.table_ref, ...), custom_call_target="tpu_custom_call", output_to_operand_aliasing={{0}: (6, {}), {1}: (7, {}), {2}: (8, {}), {3}: (9, {})} | custom-call | tf_op jit(solution)/shard_map/pallas_call | solution.py:118
  57.0 0.1 collective-permute-start.12
  57.1 3.2 %collective-permute-start.13 = (bf16[20,336,128]{2,1,0:T(8,128)(2,1)}, bf16[20,336,128]{2,1,0:T(8,128)(2,1)S(1)}, u32[]{:S(2)}, u32[]{:S(2)}) collective-permute-start(bf16[20,336,128]{2,1,0:T(8,128)(2,1)} %get-tuple-element.46), channel_id=1, source_target_pairs={{0,24},{8,0},{16,8},{24,16},{32,56},{40,32},{48,40},{56,48},{64,88... | collective-permute-start | bytes 5160968 | tf_op jit(solution)/shard_map/ppermute | solution.py:29
  60.3 2.1 %collective-permute-start.14 = (bf16[20,336,128]{2,1,0:T(8,128)(2,1)}, bf16[20,336,128]{2,1,0:T(8,128)(2,1)}, u32[]{:S(2)}, u32[]{:S(2)}) collective-permute-start(bf16[20,336,128]{2,1,0:T(8,128)(2,1)} %get-tuple-element.47), channel_id=1, source_target_pairs={{0,32},{8,40},{16,48},{24,56},{32,64},{40,72},{48,80},{56,88},{64,... | collective-permute-start | bytes 5160968 | tf_op jit(solution)/shard_map/ppermute | solution.py:29
  62.4 1.7 collective-permute-start.15
  64.1 0.8 copy.18
  64.9 0.7 reshape.55.cols_ref
  65.6 1.6 reshape.54.rank_ref
  67.2 1.3 dynamic_slice.3
  68.5 4.4 %shard_map.77 = (bf16[20,336,128]{2,1,0:T(8,128)(2,1)}, bf16[20,336,128]{2,1,0:T(8,128)(2,1)}) custom-call(s32[1]{0:T(128)} %bitcast.me_ref, s32[1280]{0:T(1024)} %reshape.53.table_ref, bf16[5,336,128]{2,1,0:T(8,128)(2,1)} %get-tuple-element.35.refs_0_, bf16[5,336,128]{2,1,0:T(8,128)(2,1)} %get-tuple-element.37.refs_1_, ...), custom_call_target="tpu_custom_call" | custom-call | tf_op jit(solution)/shard_map/pallas_call | solution.py:118
  72.9 20.7 %collective-permute-done.12.refs_16_ = bf16[20,336,128]{2,1,0:T(8,128)(2,1)S(1)} collective-permute-done((bf16[20,336,128]{2,1,0:T(8,128)(2,1)}, bf16[20,336,128]{2,1,0:T(8,128)(2,1)S(1)}, u32[]{:S(2)}, u32[]{:S(2)}) %collective-permute-start.12) | collective-permute-done | bytes 1720352 | tf_op jit(solution)/shard_map/ppermute | solution.py:29
  93.6 17.8 %collective-permute-done.13.refs_17_ = bf16[20,336,128]{2,1,0:T(8,128)(2,1)S(1)} collective-permute-done((bf16[20,336,128]{2,1,0:T(8,128)(2,1)}, bf16[20,336,128]{2,1,0:T(8,128)(2,1)S(1)}, u32[]{:S(2)}, u32[]{:S(2)}) %collective-permute-start.13) | collective-permute-done | bytes 1720352 | tf_op jit(solution)/shard_map/ppermute | solution.py:29
  111.4 0.0 collective-permute-done.14.refs_18_
  111.4 0.0 collective-permute-done.15.refs_19_
  111.4 0.1 collective-permute-start.16
  111.5 1.2 copy-done.11
  112.7 5.1 %collective-permute-start.17 = (bf16[20,336,128]{2,1,0:T(8,128)(2,1)}, bf16[20,336,128]{2,1,0:T(8,128)(2,1)S(1)}, u32[]{:S(2)}, u32[]{:S(2)}) collective-permute-start(bf16[20,336,128]{2,1,0:T(8,128)(2,1)} %get-tuple-element.54), channel_id=1, source_target_pairs={{0,64},{8,72},{16,80},{24,88},{32,96},{40,104},{48,112},{56,120},{... | collective-permute-start | bytes 5160968 | tf_op jit(solution)/shard_map/ppermute | solution.py:29
  117.8 20.5 %shard_map.76 = (f32[4,336,256]{2,1,0:T(8,128)}, s32[320]{0:T(512)}, bf16[1024,1024]{1,0:T(8,128)(2,1)}) custom-call(s32[1]{0:T(128)} %bitcast.me_ref, s32[1280]{0:T(1024)} %reshape.53.table_ref, s32[2560]{0:T(1024)} %reshape.54.rank_ref, s32[2560]{0:T(1024)} %reshape.55.cols_ref, bf16[5,336,128]{2,1,0:T(8,128)(2,1)} %get-tuple-element.35.refs_0_, ...), custom_call_target="tpu_custom_call" | custom-call | flops 7046430720 | bytes 37748736 | tf_op jit(solution)/shard_map/pallas_call | solution.py:219
  138.3 0.0 collective-permute-done.16.lo_ref
  138.3 1.2 copy-done.8
  139.5 0.5 copy-done.9
  140.0 13.8 %shard_map.78 = bf16[1024,336]{1,0:T(8,128)(2,1)} custom-call(s32[320]{0:T(512)} %get-tuple-element.49.use_ref, bf16[20,336,128]{2,1,0:T(8,128)(2,1)} %copy-done.8, bf16[20,336,128]{2,1,0:T(8,128)(2,1)} %copy-done.9, bf16[4,40,256,256]{3,2,1,0:T(8,128)(2,1)} %all-gather.2.cloned.1.call-done.refs_20_.f_ref, f32[4,336,256]{2,1,0:T(8,128)} %get-tuple-element.55.acc_ref, ...), custom_call_target="tpu_custom_call" | custom-call | flops 3523215360 | bytes 29360128 | tf_op jit(solution)/shard_map/pallas_call | solution.py:295
  153.8 18.1 %all_to_all.5 = bf16[16,64,336]{2,1,0:T(8,128)(2,1)S(1)} all-to-all(bf16[16,64,336]{2,1,0:T(8,128)(2,1)} %bitcast.6), channel_id=1, replica_groups=mesh['site'=16,'scen'=8] {'site'}, dimensions={0} | all-to-all | bytes 1376256 | tf_op jit(solution)/shard_map/all_to_all | solution.py:355
  171.9 0.8 convert_reduce_fusion
  (26 shorter events, 0.1 us)
Async XLA Ops:
  6.5 10.2 %copy-start.12 = (s32[64,40]{0,1:T(8,128)S(1)}, s32[64,40]{0,1:T(8,128)}, u32[]{:S(2)}) copy-start(s32[64,40]{0,1:T(8,128)} %param.8) | copy-start | bytes 30724
  6.5 111.3 %all-gather.2.cloned.1.call-start = ((), (), s32[]{:S(2)}) async-start(), calls=%async_computation.1 | async-start | bytes 23592960 | tf_op jit(solution)/shard_map/all_gather | solution.py:312
  10.2 13.1 %collective-permute-start = (bf16[5,336,128]{2,1,0:T(8,128)(2,1)}, bf16[5,336,128]{2,1,0:T(8,128)(2,1)S(1)}, u32[]{:S(2)}, u32[]{:S(2)}) collective-permute-start(bf16[5,336,128]{2,1,0:T(8,128)(2,1)} %get-tuple-element.35.refs_0_), channel_id=1, source_target_pairs={{0,32},{8,40},{16,48},{24,56},{32,64},{40,72},{48,80},{56,88},{64,... | collective-permute-start | bytes 1290248 | tf_op jit(solution)/shard_map/ppermute | solution.py:29
  11.7 12.8 %collective-permute-start.1 = (bf16[5,336,128]{2,1,0:T(8,128)(2,1)}, bf16[5,336,128]{2,1,0:T(8,128)(2,1)S(1)}, u32[]{:S(2)}, u32[]{:S(2)}) collective-permute-start(bf16[5,336,128]{2,1,0:T(8,128)(2,1)} %get-tuple-element.38.refs_6_.refs_8_), channel_id=1, source_target_pairs={{0,8},{8,16},{16,24},{24,0},{32,40},{40,48},{48,56},{56,32},{64,72... | collective-permute-start | bytes 1290248 | tf_op jit(solution)/shard_map/ppermute | solution.py:29
  13.3 11.3 %collective-permute-start.2 = (bf16[5,336,128]{2,1,0:T(8,128)(2,1)}, bf16[5,336,128]{2,1,0:T(8,128)(2,1)S(1)}, u32[]{:S(2)}, u32[]{:S(2)}) collective-permute-start(bf16[5,336,128]{2,1,0:T(8,128)(2,1)} %get-tuple-element.37.refs_1_), channel_id=1, source_target_pairs={{0,96},{8,104},{16,112},{24,120},{32,0},{40,8},{48,16},{56,24},{64... | collective-permute-start | bytes 1290248 | tf_op jit(solution)/shard_map/ppermute | solution.py:29
  15.1 11.0 %collective-permute-start.3 = (bf16[5,336,128]{2,1,0:T(8,128)(2,1)}, bf16[5,336,128]{2,1,0:T(8,128)(2,1)S(1)}, u32[]{:S(2)}, u32[]{:S(2)}) collective-permute-start(bf16[5,336,128]{2,1,0:T(8,128)(2,1)} %get-tuple-element.40.refs_7_.refs_9_), channel_id=1, source_target_pairs={{0,24},{8,0},{16,8},{24,16},{32,56},{40,32},{48,40},{56,48},{64,88... | collective-permute-start | bytes 1290248 | tf_op jit(solution)/shard_map/ppermute | solution.py:29
  23.3 24.0 %copy-start.4 = (bf16[5,336,128]{2,1,0:T(8,128)(2,1)}, bf16[5,336,128]{2,1,0:T(8,128)(2,1)S(1)}, u32[]{:S(2)}) copy-start(bf16[5,336,128]{2,1,0:T(8,128)(2,1)S(1)} %collective-permute-done.refs_4_.refs_6_) | copy-start | bytes 1290244
  24.6 22.7 %copy-start.5 = (bf16[5,336,128]{2,1,0:T(8,128)(2,1)}, bf16[5,336,128]{2,1,0:T(8,128)(2,1)S(1)}, u32[]{:S(2)}) copy-start(bf16[5,336,128]{2,1,0:T(8,128)(2,1)S(1)} %collective-permute-done.1.refs_10_.refs_14_) | copy-start | bytes 1290244
  24.6 22.7 %copy-start.6 = (bf16[5,336,128]{2,1,0:T(8,128)(2,1)}, bf16[5,336,128]{2,1,0:T(8,128)(2,1)S(1)}, u32[]{:S(2)}) copy-start(bf16[5,336,128]{2,1,0:T(8,128)(2,1)S(1)} %collective-permute-done.2.refs_3_) | copy-start | bytes 1290244
  26.1 21.3 %copy-start.7 = (bf16[5,336,128]{2,1,0:T(8,128)(2,1)}, bf16[5,336,128]{2,1,0:T(8,128)(2,1)S(1)}, u32[]{:S(2)}) copy-start(bf16[5,336,128]{2,1,0:T(8,128)(2,1)S(1)} %collective-permute-done.3.refs_9_.refs_11_) | copy-start | bytes 1290244
  26.1 10.2 %collective-permute-start.4 = (bf16[5,336,128]{2,1,0:T(8,128)(2,1)}, bf16[5,336,128]{2,1,0:T(8,128)(2,1)}, u32[]{:S(2)}, u32[]{:S(2)}) collective-permute-start(bf16[5,336,128]{2,1,0:T(8,128)(2,1)} %get-tuple-element.35.refs_0_), channel_id=1, source_target_pairs={{0,96},{8,104},{16,112},{24,120},{32,0},{40,8},{48,16},{56,24},{64... | collective-permute-start | bytes 1290248 | tf_op jit(solution)/shard_map/ppermute | solution.py:29
  27.6 14.4 %collective-permute-start.7 = (bf16[5,336,128]{2,1,0:T(8,128)(2,1)}, bf16[5,336,128]{2,1,0:T(8,128)(2,1)}, u32[]{:S(2)}, u32[]{:S(2)}) collective-permute-start(bf16[5,336,128]{2,1,0:T(8,128)(2,1)} %get-tuple-element.37.refs_1_), channel_id=1, source_target_pairs={{0,32},{8,40},{16,48},{24,56},{32,64},{40,72},{48,80},{56,88},{64,... | collective-permute-start | bytes 1290248 | tf_op jit(solution)/shard_map/ppermute | solution.py:29
  28.1 13.9 %collective-permute-start.8 = (bf16[5,336,128]{2,1,0:T(8,128)(2,1)}, bf16[5,336,128]{2,1,0:T(8,128)(2,1)}, u32[]{:S(2)}, u32[]{:S(2)}) collective-permute-start(bf16[5,336,128]{2,1,0:T(8,128)(2,1)} %get-tuple-element.38.refs_6_.refs_8_), channel_id=1, source_target_pairs={{0,24},{8,0},{16,8},{24,16},{32,56},{40,32},{48,40},{56,48},{64,88... | collective-permute-start | bytes 1290248 | tf_op jit(solution)/shard_map/ppermute | solution.py:29
  32.7 19.9 %collective-permute-start.5 = (bf16[5,336,128]{2,1,0:T(8,128)(2,1)S(1)}, bf16[5,336,128]{2,1,0:T(8,128)(2,1)S(1)}, u32[]{:S(2)}, u32[]{:S(2)}) collective-permute-start(bf16[5,336,128]{2,1,0:T(8,128)(2,1)S(1)} %collective-permute-done.refs_4_.refs_6_), channel_id=1, source_target_pairs={{0,32},{8,40},{16,48},{24,56},{32,64},{40,72},{48,80},{56,88},{64,... | collective-permute-start | bytes 1290248 | tf_op jit(solution)/shard_map/ppermute | solution.py:29
  32.9 14.4 %collective-permute-start.11 = (bf16[5,336,128]{2,1,0:T(8,128)(2,1)}, bf16[5,336,128]{2,1,0:T(8,128)(2,1)}, u32[]{:S(2)}, u32[]{:S(2)}) collective-permute-start(bf16[5,336,128]{2,1,0:T(8,128)(2,1)} %get-tuple-element.40.refs_7_.refs_9_), channel_id=1, source_target_pairs={{0,8},{8,16},{16,24},{24,0},{32,40},{40,48},{48,56},{56,32},{64,72... | collective-permute-start | bytes 1290248 | tf_op jit(solution)/shard_map/ppermute | solution.py:29
  36.3 16.4 %collective-permute-start.9 = (bf16[5,336,128]{2,1,0:T(8,128)(2,1)S(1)}, bf16[5,336,128]{2,1,0:T(8,128)(2,1)S(1)}, u32[]{:S(2)}, u32[]{:S(2)}) collective-permute-start(bf16[5,336,128]{2,1,0:T(8,128)(2,1)S(1)} %collective-permute-done.1.refs_10_.refs_14_), channel_id=1, source_target_pairs={{0,8},{8,16},{16,24},{24,0},{32,40},{40,48},{48,56},{56,32},{64,72... | collective-permute-start | bytes 1290248 | tf_op jit(solution)/shard_map/ppermute | solution.py:29
  42.0 10.6 %collective-permute-start.6 = (bf16[5,336,128]{2,1,0:T(8,128)(2,1)S(1)}, bf16[5,336,128]{2,1,0:T(8,128)(2,1)S(1)}, u32[]{:S(2)}, u32[]{:S(2)}) collective-permute-start(bf16[5,336,128]{2,1,0:T(8,128)(2,1)S(1)} %collective-permute-done.2.refs_3_), channel_id=1, source_target_pairs={{0,96},{8,104},{16,112},{24,120},{32,0},{40,8},{48,16},{56,24},{64... | collective-permute-start | bytes 1290248 | tf_op jit(solution)/shard_map/ppermute | solution.py:29
  42.0 10.7 %collective-permute-start.10 = (bf16[5,336,128]{2,1,0:T(8,128)(2,1)S(1)}, bf16[5,336,128]{2,1,0:T(8,128)(2,1)S(1)}, u32[]{:S(2)}, u32[]{:S(2)}) collective-permute-start(bf16[5,336,128]{2,1,0:T(8,128)(2,1)S(1)} %collective-permute-done.3.refs_9_.refs_11_), channel_id=1, source_target_pairs={{0,24},{8,0},{16,8},{24,16},{32,56},{40,32},{48,40},{56,48},{64,88... | collective-permute-start | bytes 1290248 | tf_op jit(solution)/shard_map/ppermute | solution.py:29
  52.6 0.8 copy-start
  52.6 0.9 copy-start.2
  52.7 1.0 copy-start.1
  52.7 1.1 copy-start.3
  57.0 36.5 %collective-permute-start.12 = (bf16[20,336,128]{2,1,0:T(8,128)(2,1)}, bf16[20,336,128]{2,1,0:T(8,128)(2,1)S(1)}, u32[]{:S(2)}, u32[]{:S(2)}) collective-permute-start(bf16[20,336,128]{2,1,0:T(8,128)(2,1)} %get-tuple-element.45), channel_id=1, source_target_pairs={{0,8},{8,16},{16,24},{24,0},{32,40},{40,48},{48,56},{56,32},{64,72... | collective-permute-start | bytes 5160968 | tf_op jit(solution)/shard_map/ppermute | solution.py:29
  57.1 54.3 %collective-permute-start.13 = (bf16[20,336,128]{2,1,0:T(8,128)(2,1)}, bf16[20,336,128]{2,1,0:T(8,128)(2,1)S(1)}, u32[]{:S(2)}, u32[]{:S(2)}) collective-permute-start(bf16[20,336,128]{2,1,0:T(8,128)(2,1)} %get-tuple-element.46), channel_id=1, source_target_pairs={{0,24},{8,0},{16,8},{24,16},{32,56},{40,32},{48,40},{56,48},{64,88... | collective-permute-start | bytes 5160968 | tf_op jit(solution)/shard_map/ppermute | solution.py:29
  60.3 51.1 %collective-permute-start.14 = (bf16[20,336,128]{2,1,0:T(8,128)(2,1)}, bf16[20,336,128]{2,1,0:T(8,128)(2,1)}, u32[]{:S(2)}, u32[]{:S(2)}) collective-permute-start(bf16[20,336,128]{2,1,0:T(8,128)(2,1)} %get-tuple-element.47), channel_id=1, source_target_pairs={{0,32},{8,40},{16,48},{24,56},{32,64},{40,72},{48,80},{56,88},{64,... | collective-permute-start | bytes 5160968 | tf_op jit(solution)/shard_map/ppermute | solution.py:29
  62.4 49.0 %collective-permute-start.15 = (bf16[20,336,128]{2,1,0:T(8,128)(2,1)}, bf16[20,336,128]{2,1,0:T(8,128)(2,1)}, u32[]{:S(2)}, u32[]{:S(2)}) collective-permute-start(bf16[20,336,128]{2,1,0:T(8,128)(2,1)} %get-tuple-element.48), channel_id=1, source_target_pairs={{0,96},{8,104},{16,112},{24,120},{32,0},{40,8},{48,16},{56,24},{64... | collective-permute-start | bytes 5160968 | tf_op jit(solution)/shard_map/ppermute | solution.py:29
  93.6 17.8 %copy-start.10 = (bf16[20,336,128]{2,1,0:T(8,128)(2,1)}, bf16[20,336,128]{2,1,0:T(8,128)(2,1)S(1)}, u32[]{:S(2)}) copy-start(bf16[20,336,128]{2,1,0:T(8,128)(2,1)S(1)} %collective-permute-done.12.refs_16_) | copy-start | bytes 5160964
  111.4 1.3 copy-start.11
  111.4 26.8 %collective-permute-start.16 = (bf16[20,336,128]{2,1,0:T(8,128)(2,1)}, bf16[20,336,128]{2,1,0:T(8,128)(2,1)S(1)}, u32[]{:S(2)}, u32[]{:S(2)}) collective-permute-start(bf16[20,336,128]{2,1,0:T(8,128)(2,1)} %get-tuple-element.52), channel_id=1, source_target_pairs={{0,16},{8,24},{16,0},{24,8},{32,48},{40,56},{48,32},{56,40},{64,80... | collective-permute-start | bytes 5160968 | tf_op jit(solution)/shard_map/ppermute | solution.py:29
  112.7 25.6 %collective-permute-start.17 = (bf16[20,336,128]{2,1,0:T(8,128)(2,1)}, bf16[20,336,128]{2,1,0:T(8,128)(2,1)S(1)}, u32[]{:S(2)}, u32[]{:S(2)}) collective-permute-start(bf16[20,336,128]{2,1,0:T(8,128)(2,1)} %get-tuple-element.54), channel_id=1, source_target_pairs={{0,64},{8,72},{16,80},{24,88},{32,96},{40,104},{48,112},{56,120},{... | collective-permute-start | bytes 5160968 | tf_op jit(solution)/shard_map/ppermute | solution.py:29
  138.3 1.2 copy-start.8
  138.3 1.7 copy-start.9
Sparse Core Ops, SparseCore 0:
  9.1 103.8 all-gather.1

commit v4 on v3

--- a/solution.py
+++ b/solution.py
@@ -142,7 +142,7 @@
 
 
 def early_kernel(me_ref, table_ref, rank_ref, cols_ref, *refs):
-    held, sent, f_ref, bus_ref, acc_ref, use_ref, onehot_ref, zlo, zhi, sem = (
+    held, sent, f_ref, acc_ref, use_ref, zlo, zhi, sem = (
         pairs(refs[:16]), refs[16:20], *refs[20:]
     )
     r = pl.program_id(0)
@@ -190,11 +190,24 @@
         term = lax.dot_general(z, f_ref[0, t], NT, preferred_element_type=jnp.float32)
         total = term if total is None else total + term
     acc_ref[0] = total
+
+
+def onehot_kernel(bus_ref, onehot_ref):
     buses = lax.broadcasted_iota(jnp.int32, (BUSES, BLK), 0)
     onehot_ref[...] = jnp.where(buses == bus_ref[0], 1.0, 0.0).astype(jnp.bfloat16)
 
 
-def early(scalars, arrays, factor, bus):
+def onehot_of(bus):
+    return pl.pallas_call(
+        onehot_kernel,
+        grid=(RB_DEV,),
+        in_specs=[pl.BlockSpec((1, 1, BLK), lambda r: (r, 0, 0))],
+        out_specs=pl.BlockSpec((BUSES, BLK), lambda r: (0, r)),
+        out_shape=jax.ShapeDtypeStruct((BUSES, RB_DEV * BLK), jnp.bfloat16),
+    )(bus)
+
+
+def early(scalars, arrays, factor):
     width = arrays[0].shape[1]
     slots = SIDE * SIDE * SLOTS
     grid_spec = pltpu.PrefetchScalarGridSpec(
@@ -203,12 +216,10 @@
         in_specs=[ANY] * len(arrays)
         + [
             pl.BlockSpec((1, NZ, BLK, BLK), lambda r, *_: (r, 0, 0, 0)),
-            pl.BlockSpec((1, 1, BLK), lambda r, *_: (r, 0, 0)),
         ],
         out_specs=[
             pl.BlockSpec((1, width, BLK), lambda r, *_: (r, 0, 0)),
             pl.BlockSpec(memory_space=pltpu.SMEM),
-            pl.BlockSpec((BUSES, BLK), lambda r, *_: (0, r)),
         ],
         scratch_shapes=[
             pltpu.VMEM((slots, width, HALF), jnp.bfloat16),
@@ -222,13 +233,12 @@
         out_shape=[
             jax.ShapeDtypeStruct((RB_DEV, width, BLK), jnp.float32),
             jax.ShapeDtypeStruct((RB_DEV * slots,), jnp.int32),
-            jax.ShapeDtypeStruct((BUSES, RB_DEV * BLK), jnp.bfloat16),
         ],
         compiler_params=pltpu.CompilerParams(vmem_limit_bytes=ALL_VMEM),
         cost_estimate=pl.CostEstimate(
             flops=2 * RB_DEV * NZ * BLK * BLK * width, bytes_accessed=36 << 20, transcendentals=0
         ),
-    )(*scalars, *arrays, factor, bus)
+    )(*scalars, *arrays, factor)
 
 
 def late_kernel(use_ref, lo_ref, hi_ref, f_ref, acc_ref, temporal_ref, cap_ref, spr_ref, onehot_ref, *refs):
@@ -344,13 +354,14 @@
     flat = (rank.reshape(-1), pattern.reshape(-1))
     held = RB_DEV * BLK
     bus = lax.dynamic_slice_in_dim(bus_map, me * held, held, 0)
-    out = picked((2,), (0, 1, 2, 3), (after(index, out[0], *flat, bus), table), lines)
+    onehot = onehot_of(bus.reshape(RB_DEV, 1, BLK))
+    out = picked((2,), (0, 1, 2, 3), (after(index, out[0], *flat, onehot), table), lines)
     opposite = [step(after(b, *sent), 1 - axis, 2) for axis, b in enumerate(out)]
     arrays = [p for line in lines for pair in line for p in pair] + sent
     shape = (RB_DEV, 1, BLK)
     scalars = (index, table, *flat)
     vectors = (capacity.reshape(shape), spread.reshape(shape))
-    acc, use, onehot = early(scalars, arrays, portion, bus.reshape(shape))
+    acc, use = early(scalars, arrays, portion)
     power = late(use, opposite, portion, acc, temporal, vectors, onehot)
     tiles = lax.all_to_all(power.reshape(sites, -1, power.shape[1]), "site", 0, 0, tiled=True)
     return jnp.sum(tiles.astype(jnp.float32), axis=0)

time: 181 us -> 181 us (level)
  Pallas kernels: 50.1 us -> 52.9 us
  waiting for transfers between devices: 57.7 us -> 55.3 us
    pallas_call x0 -> x1, Pallas kernels: none -> 3.21 us  [onehot_of(): pl.pallas_call(onehot_kernel, grid=(RB_DEV,), in_specs=[pl.BlockSpec((1,...]
    ppermute x18, waiting for transfers between devices: 57 us -> 54.5 us  [shift(): return lax.ppermute(value, 'site', pairs)]
  transfers between devices with their start and end apart: 19 -> 19, of which waited for: 8 -> 9; matrix products, arithmetic and copies ran while one was open for 4% -> 4% of each run, Pallas kernels for 20% -> 22%
where the time goes in v4:
time: 181 us; the launch traced here: 180 us
  waiting for transfers between devices  55.3 us (31%)
  Pallas kernels  52.9 us (29%)
  starting transfers between devices  28.2 us (16%)
  blocking collectives  18.9 us (10%)
  between operations  13.6 us (8%)
  local copies, waits for them, and re-layouts  9.56 us (5%)
    ppermute x18, waiting for transfers between devices, shift(): return lax.ppermute(value, 'site', pairs)  54.5 us
    ppermute x18, starting transfers between devices, shift(): return lax.ppermute(value, 'site', pairs)  28.2 us
    pallas_call x1, Pallas kernels, early(): pl.pallas_call(early_kernel, grid_spec=grid_spec, out_shape=[jax.ShapeDty...  19.6 us
    all_to_all x1, blocking collectives, shards(): lax.all_to_all(power.reshape(sites, -1, power.shape[1]), 'site', 0, 0, ti...  18.9 us
    pallas_call x1, Pallas kernels, late(): pl.pallas_call(late_kernel, grid_spec=grid_spec, out_shape=jax.ShapeDtype...  13.9 us
    pallas_call x3, Pallas kernels, picked(): pl.pallas_call(functools.partial(pick_kernel, hops, holders, bool(begun))...  13.3 us
    unnamed x27, local copies, waits for them, and re-layouts  3.64 us
  transfers between devices with their start and end apart: 19, of which 9 were waited for; matrix products, arithmetic and copies ran while one was open for 4% of the time, Pallas kernels for 22%

profile of v4, /device:TPU:64, one launch (start us, length us, event | category | flops | bytes accessed | tf_op | source)
XLA Modules:
  0.0 180.0 jit_solution(5991333712655791548)
XLA Ops:
  6.5 0.7 all-gather.2.cloned.1.call-update
  7.3 3.0 %shard_map.73 = (bf16[5,336,128]{2,1,0:T(8,128)(2,1)}, bf16[5,336,128]{2,1,0:T(8,128)(2,1)}, bf16[5,336,128]{2,1,0:T(8,128)(2,1)}, bf16[5,336,128]{2,1,0:T(8,128)(2,1)}) custom-call(bf16[336,2560]{1,0:T(8,128)(2,1)} %bitcast.7), custom_call_target="tpu_custom_call" | custom-call | tf_op jit(solution)/shard_map/pallas_call | solution.py:53
  10.2 1.5 collective-permute-start
  11.7 1.6 collective-permute-start.1
  13.3 1.7 collective-permute-start.2
  15.0 1.7 collective-permute-start.3
  16.7 0.1 copy.14
  16.8 0.1 eq.39
  16.8 0.5 fusion
  17.4 0.1 reshape.60
  17.5 5.8 %collective-permute-done.refs_4_.refs_6_ = bf16[5,336,128]{2,1,0:T(8,128)(2,1)S(1)} collective-permute-done((bf16[5,336,128]{2,1,0:T(8,128)(2,1)}, bf16[5,336,128]{2,1,0:T(8,128)(2,1)S(1)}, u32[]{:S(2)}, u32[]{:S(2)}) %collective-permute-start) | collective-permute-done | bytes 430112 | tf_op jit(solution)/shard_map/ppermute | solution.py:29
  23.3 1.3 collective-permute-done.1.refs_10_.refs_14_
  24.6 0.0 collective-permute-done.2.refs_3_
  24.6 1.5 collective-permute-done.3.refs_9_.refs_11_
  26.0 1.6 collective-permute-start.4
  27.6 0.5 collective-permute-start.7
  28.1 2.9 %collective-permute-start.8 = (bf16[5,336,128]{2,1,0:T(8,128)(2,1)}, bf16[5,336,128]{2,1,0:T(8,128)(2,1)}, u32[]{:S(2)}, u32[]{:S(2)}) collective-permute-start(bf16[5,336,128]{2,1,0:T(8,128)(2,1)} %get-tuple-element.37.refs_6_.refs_8_), channel_id=1, source_target_pairs={{0,24},{8,0},{16,8},{24,16},{32,56},{40,32},{48,40},{56,48},{64,88... | collective-permute-start | bytes 1290248 | tf_op jit(solution)/shard_map/ppermute | solution.py:29
  31.0 0.2 copy.16
  31.2 0.2 copy.15
  31.4 0.2 multiply_reduce_fusion
  31.6 0.1 select_reduce_fusion
  31.7 0.2 copy.17
  31.8 0.8 reshape.53.table_ref
  32.6 0.3 collective-permute-start.5
  32.9 0.0 collective-permute-start.11
  32.9 3.3 %collective-permute-done.4.refs_2_ = bf16[5,336,128]{2,1,0:T(8,128)(2,1)} collective-permute-done((bf16[5,336,128]{2,1,0:T(8,128)(2,1)}, bf16[5,336,128]{2,1,0:T(8,128)(2,1)}, u32[]{:S(2)}, u32[]{:S(2)}) %collective-permute-start.4) | collective-permute-done | bytes 430112 | tf_op jit(solution)/shard_map/ppermute | solution.py:29
  36.2 1.6 collective-permute-start.9
  37.8 4.2 %collective-permute-done.7.refs_5_.refs_7_ = bf16[5,336,128]{2,1,0:T(8,128)(2,1)} collective-permute-done((bf16[5,336,128]{2,1,0:T(8,128)(2,1)}, bf16[5,336,128]{2,1,0:T(8,128)(2,1)}, u32[]{:S(2)}, u32[]{:S(2)}) %collective-permute-start.7) | collective-permute-done | bytes 430112 | tf_op jit(solution)/shard_map/ppermute | solution.py:29
  42.0 0.0 collective-permute-start.6
  42.0 0.0 collective-permute-done.8.refs_8_.refs_10_
  42.0 2.9 %collective-permute-start.10 = (bf16[5,336,128]{2,1,0:T(8,128)(2,1)S(1)}, bf16[5,336,128]{2,1,0:T(8,128)(2,1)S(1)}, u32[]{:S(2)}, u32[]{:S(2)}) collective-permute-start(bf16[5,336,128]{2,1,0:T(8,128)(2,1)S(1)} %collective-permute-done.3.refs_9_.refs_11_), channel_id=1, source_target_pairs={{0,24},{8,0},{16,8},{24,16},{32,56},{40,32},{48,40},{56,48},{64,88... | collective-permute-start | bytes 1290248 | tf_op jit(solution)/shard_map/ppermute | solution.py:29
  44.9 2.4 %collective-permute-done.11.refs_11_.refs_15_ = bf16[5,336,128]{2,1,0:T(8,128)(2,1)} collective-permute-done((bf16[5,336,128]{2,1,0:T(8,128)(2,1)}, bf16[5,336,128]{2,1,0:T(8,128)(2,1)}, u32[]{:S(2)}, u32[]{:S(2)}) %collective-permute-start.11) | collective-permute-done | bytes 430112 | tf_op jit(solution)/shard_map/ppermute | solution.py:29
  47.3 5.5 %shard_map.74 = (bf16[20,336,128]{2,1,0:T(8,128)(2,1)}, bf16[20,336,128]{2,1,0:T(8,128)(2,1)}, bf16[20,336,128]{2,1,0:T(8,128)(2,1)}, bf16[20,336,128]{2,1,0:T(8,128)(2,1)}) custom-call(s32[1]{0:T(128)} %bitcast.me_ref, s32[1280]{0:T(1024)} %reshape.53.table_ref, bf16[5,336,128]{2,1,0:T(8,128)(2,1)} %get-tuple-element.34.refs_0_, ...), custom_call_target="tpu_custom_call" | custom-call | tf_op jit(solution)/shard_map/pallas_call | solution.py:118
  52.8 0.0 collective-permute-done.5.refs_0_.refs_4_
  52.9 0.0 collective-permute-done.6.refs_1_.refs_5_
  52.9 0.0 collective-permute-done.9.refs_2_.refs_12_
  52.9 0.7 copy-done
  53.6 0.2 copy-done.2
  53.8 0.2 copy-done.1
  53.9 0.2 copy-done.3
  54.1 3.5 %shard_map.75 = (bf16[20,336,128]{2,1,0:T(8,128)(2,1)}, bf16[20,336,128]{2,1,0:T(8,128)(2,1)}, bf16[20,336,128]{2,1,0:T(8,128)(2,1)}, bf16[20,336,128]{2,1,0:T(8,128)(2,1)}) custom-call(s32[1]{0:T(128)} %bitcast.me_ref, s32[1280]{0:T(1024)} %reshape.53.table_ref, ...), custom_call_target="tpu_custom_call", output_to_operand_aliasing={{0}: (6, {}), {1}: (7, {}), {2}: (8, {}), {3}: (9, {})} | custom-call | tf_op jit(solution)/shard_map/pallas_call | solution.py:118
  57.6 0.1 collective-permute-start.12
  57.7 3.2 %collective-permute-start.13 = (bf16[20,336,128]{2,1,0:T(8,128)(2,1)}, bf16[20,336,128]{2,1,0:T(8,128)(2,1)S(1)}, u32[]{:S(2)}, u32[]{:S(2)}) collective-permute-start(bf16[20,336,128]{2,1,0:T(8,128)(2,1)} %get-tuple-element.45), channel_id=1, source_target_pairs={{0,24},{8,0},{16,8},{24,16},{32,56},{40,32},{48,40},{56,48},{64,88... | collective-permute-start | bytes 5160968 | tf_op jit(solution)/shard_map/ppermute | solution.py:29
  60.9 1.8 %collective-permute-start.14 = (bf16[20,336,128]{2,1,0:T(8,128)(2,1)}, bf16[20,336,128]{2,1,0:T(8,128)(2,1)}, u32[]{:S(2)}, u32[]{:S(2)}) collective-permute-start(bf16[20,336,128]{2,1,0:T(8,128)(2,1)} %get-tuple-element.46), channel_id=1, source_target_pairs={{0,32},{8,40},{16,48},{24,56},{32,64},{40,72},{48,80},{56,88},{64,... | collective-permute-start | bytes 5160968 | tf_op jit(solution)/shard_map/ppermute | solution.py:29
  62.8 1.5 collective-permute-start.15
  64.3 0.8 copy.18
  65.1 0.7 reshape.55.cols_ref
  65.8 1.6 reshape.54.rank_ref
  67.4 1.3 dynamic_slice.3
  68.7 3.2 %shard_map.77.onehot_ref = bf16[1024,1024]{1,0:T(8,128)(2,1)} custom-call(s32[4,1,256]{2,1,0:T(1,128)} %bitcast.8), custom_call_target="tpu_custom_call" | custom-call | tf_op jit(solution)/shard_map/pallas_call | solution.py:201
  71.9 4.3 %shard_map.78 = (bf16[20,336,128]{2,1,0:T(8,128)(2,1)}, bf16[20,336,128]{2,1,0:T(8,128)(2,1)}) custom-call(s32[1]{0:T(128)} %bitcast.me_ref, s32[1280]{0:T(1024)} %reshape.53.table_ref, bf16[5,336,128]{2,1,0:T(8,128)(2,1)} %get-tuple-element.34.refs_0_, bf16[5,336,128]{2,1,0:T(8,128)(2,1)} %get-tuple-element.36.refs_1_, ...), custom_call_target="tpu_custom_call" | custom-call | tf_op jit(solution)/shard_map/pallas_call | solution.py:118
  76.2 17.7 %collective-permute-done.12.refs_16_ = bf16[20,336,128]{2,1,0:T(8,128)(2,1)S(1)} collective-permute-done((bf16[20,336,128]{2,1,0:T(8,128)(2,1)}, bf16[20,336,128]{2,1,0:T(8,128)(2,1)S(1)}, u32[]{:S(2)}, u32[]{:S(2)}) %collective-permute-start.12) | collective-permute-done | bytes 1720352 | tf_op jit(solution)/shard_map/ppermute | solution.py:29
  93.9 17.8 %collective-permute-done.13.refs_17_ = bf16[20,336,128]{2,1,0:T(8,128)(2,1)S(1)} collective-permute-done((bf16[20,336,128]{2,1,0:T(8,128)(2,1)}, bf16[20,336,128]{2,1,0:T(8,128)(2,1)S(1)}, u32[]{:S(2)}, u32[]{:S(2)}) %collective-permute-start.13) | collective-permute-done | bytes 1720352 | tf_op jit(solution)/shard_map/ppermute | solution.py:29
  111.7 0.1 collective-permute-start.16
  111.8 1.1 copy-done.11
  112.9 5.3 %collective-permute-start.17 = (bf16[20,336,128]{2,1,0:T(8,128)(2,1)}, bf16[20,336,128]{2,1,0:T(8,128)(2,1)S(1)}, u32[]{:S(2)}, u32[]{:S(2)}) collective-permute-start(bf16[20,336,128]{2,1,0:T(8,128)(2,1)} %get-tuple-element.53), channel_id=1, source_target_pairs={{0,64},{8,72},{16,80},{24,88},{32,96},{40,104},{48,112},{56,120},{... | collective-permute-start | bytes 5160968 | tf_op jit(solution)/shard_map/ppermute | solution.py:29
  118.2 19.6 %shard_map.76 = (f32[4,336,256]{2,1,0:T(8,128)}, s32[320]{0:T(512)}) custom-call(s32[1]{0:T(128)} %bitcast.me_ref, s32[1280]{0:T(1024)} %reshape.53.table_ref, s32[2560]{0:T(1024)} %reshape.54.rank_ref, s32[2560]{0:T(1024)} %reshape.55.cols_ref, bf16[5,336,128]{2,1,0:T(8,128)(2,1)} %get-tuple-element.34.refs_0_, ...), custom_call_target="tpu_custom_call" | custom-call | flops 7046430720 | bytes 37748736 | tf_op jit(solution)/shard_map/pallas_call | solution.py:230
  137.7 0.0 collective-permute-done.16.lo_ref
  137.8 0.6 collective-permute-done.17.hi_ref
  138.4 0.6 copy-done.8
  138.9 0.7 copy-done.9
  139.6 13.9 %shard_map.79 = bf16[1024,336]{1,0:T(8,128)(2,1)} custom-call(s32[320]{0:T(512)} %get-tuple-element.48.use_ref, bf16[20,336,128]{2,1,0:T(8,128)(2,1)} %copy-done.8, bf16[20,336,128]{2,1,0:T(8,128)(2,1)} %copy-done.9, bf16[4,40,256,256]{3,2,1,0:T(8,128)(2,1)} %all-gather.2.cloned.1.call-done.refs_20_.f_ref, f32[4,336,256]{2,1,0:T(8,128)} %get-tuple-element.54.acc_ref, ...), custom_call_target="tpu_custom_call" | custom-call | flops 3523215360 | bytes 29360128 | tf_op jit(solution)/shard_map/pallas_call | solution.py:305
  153.5 18.9 %all_to_all.5 = bf16[16,64,336]{2,1,0:T(8,128)(2,1)S(1)} all-to-all(bf16[16,64,336]{2,1,0:T(8,128)(2,1)} %bitcast.6), channel_id=1, replica_groups=mesh['site'=16,'scen'=8] {'site'}, dimensions={0} | all-to-all | bytes 1376256 | tf_op jit(solution)/shard_map/all_to_all | solution.py:366
  172.4 0.8 convert_reduce_fusion
  (27 shorter events, 0.1 us)
Async XLA Ops:
  6.5 10.2 %copy-start.12 = (s32[64,40]{0,1:T(8,128)S(1)}, s32[64,40]{0,1:T(8,128)}, u32[]{:S(2)}) copy-start(s32[64,40]{0,1:T(8,128)} %param.8) | copy-start | bytes 30724
  6.5 111.6 %all-gather.2.cloned.1.call-start = ((), (), s32[]{:S(2)}) async-start(), calls=%async_computation.1 | async-start | bytes 23592960 | tf_op jit(solution)/shard_map/all_gather | solution.py:322
  10.2 13.1 %collective-permute-start = (bf16[5,336,128]{2,1,0:T(8,128)(2,1)}, bf16[5,336,128]{2,1,0:T(8,128)(2,1)S(1)}, u32[]{:S(2)}, u32[]{:S(2)}) collective-permute-start(bf16[5,336,128]{2,1,0:T(8,128)(2,1)} %get-tuple-element.34.refs_0_), channel_id=1, source_target_pairs={{0,32},{8,40},{16,48},{24,56},{32,64},{40,72},{48,80},{56,88},{64,... | collective-permute-start | bytes 1290248 | tf_op jit(solution)/shard_map/ppermute | solution.py:29
  11.7 12.8 %collective-permute-start.1 = (bf16[5,336,128]{2,1,0:T(8,128)(2,1)}, bf16[5,336,128]{2,1,0:T(8,128)(2,1)S(1)}, u32[]{:S(2)}, u32[]{:S(2)}) collective-permute-start(bf16[5,336,128]{2,1,0:T(8,128)(2,1)} %get-tuple-element.37.refs_6_.refs_8_), channel_id=1, source_target_pairs={{0,8},{8,16},{16,24},{24,0},{32,40},{40,48},{48,56},{56,32},{64,72... | collective-permute-start | bytes 1290248 | tf_op jit(solution)/shard_map/ppermute | solution.py:29
  13.3 11.3 %collective-permute-start.2 = (bf16[5,336,128]{2,1,0:T(8,128)(2,1)}, bf16[5,336,128]{2,1,0:T(8,128)(2,1)S(1)}, u32[]{:S(2)}, u32[]{:S(2)}) collective-permute-start(bf16[5,336,128]{2,1,0:T(8,128)(2,1)} %get-tuple-element.36.refs_1_), channel_id=1, source_target_pairs={{0,96},{8,104},{16,112},{24,120},{32,0},{40,8},{48,16},{56,24},{64... | collective-permute-start | bytes 1290248 | tf_op jit(solution)/shard_map/ppermute | solution.py:29
  15.0 11.0 %collective-permute-start.3 = (bf16[5,336,128]{2,1,0:T(8,128)(2,1)}, bf16[5,336,128]{2,1,0:T(8,128)(2,1)S(1)}, u32[]{:S(2)}, u32[]{:S(2)}) collective-permute-start(bf16[5,336,128]{2,1,0:T(8,128)(2,1)} %get-tuple-element.39.refs_7_.refs_9_), channel_id=1, source_target_pairs={{0,24},{8,0},{16,8},{24,16},{32,56},{40,32},{48,40},{56,48},{64,88... | collective-permute-start | bytes 1290248 | tf_op jit(solution)/shard_map/ppermute | solution.py:29
  23.3 24.0 %copy-start.4 = (bf16[5,336,128]{2,1,0:T(8,128)(2,1)}, bf16[5,336,128]{2,1,0:T(8,128)(2,1)S(1)}, u32[]{:S(2)}) copy-start(bf16[5,336,128]{2,1,0:T(8,128)(2,1)S(1)} %collective-permute-done.refs_4_.refs_6_) | copy-start | bytes 1290244
  24.5 22.7 %copy-start.5 = (bf16[5,336,128]{2,1,0:T(8,128)(2,1)}, bf16[5,336,128]{2,1,0:T(8,128)(2,1)S(1)}, u32[]{:S(2)}) copy-start(bf16[5,336,128]{2,1,0:T(8,128)(2,1)S(1)} %collective-permute-done.1.refs_10_.refs_14_) | copy-start | bytes 1290244
  24.6 22.7 %copy-start.6 = (bf16[5,336,128]{2,1,0:T(8,128)(2,1)}, bf16[5,336,128]{2,1,0:T(8,128)(2,1)S(1)}, u32[]{:S(2)}) copy-start(bf16[5,336,128]{2,1,0:T(8,128)(2,1)S(1)} %collective-permute-done.2.refs_3_) | copy-start | bytes 1290244
  26.0 21.3 %copy-start.7 = (bf16[5,336,128]{2,1,0:T(8,128)(2,1)}, bf16[5,336,128]{2,1,0:T(8,128)(2,1)S(1)}, u32[]{:S(2)}) copy-start(bf16[5,336,128]{2,1,0:T(8,128)(2,1)S(1)} %collective-permute-done.3.refs_9_.refs_11_) | copy-start | bytes 1290244
  26.0 10.2 %collective-permute-start.4 = (bf16[5,336,128]{2,1,0:T(8,128)(2,1)}, bf16[5,336,128]{2,1,0:T(8,128)(2,1)}, u32[]{:S(2)}, u32[]{:S(2)}) collective-permute-start(bf16[5,336,128]{2,1,0:T(8,128)(2,1)} %get-tuple-element.34.refs_0_), channel_id=1, source_target_pairs={{0,96},{8,104},{16,112},{24,120},{32,0},{40,8},{48,16},{56,24},{64... | collective-permute-start | bytes 1290248 | tf_op jit(solution)/shard_map/ppermute | solution.py:29
  27.6 14.4 %collective-permute-start.7 = (bf16[5,336,128]{2,1,0:T(8,128)(2,1)}, bf16[5,336,128]{2,1,0:T(8,128)(2,1)}, u32[]{:S(2)}, u32[]{:S(2)}) collective-permute-start(bf16[5,336,128]{2,1,0:T(8,128)(2,1)} %get-tuple-element.36.refs_1_), channel_id=1, source_target_pairs={{0,32},{8,40},{16,48},{24,56},{32,64},{40,72},{48,80},{56,88},{64,... | collective-permute-start | bytes 1290248 | tf_op jit(solution)/shard_map/ppermute | solution.py:29
  28.1 13.9 %collective-permute-start.8 = (bf16[5,336,128]{2,1,0:T(8,128)(2,1)}, bf16[5,336,128]{2,1,0:T(8,128)(2,1)}, u32[]{:S(2)}, u32[]{:S(2)}) collective-permute-start(bf16[5,336,128]{2,1,0:T(8,128)(2,1)} %get-tuple-element.37.refs_6_.refs_8_), channel_id=1, source_target_pairs={{0,24},{8,0},{16,8},{24,16},{32,56},{40,32},{48,40},{56,48},{64,88... | collective-permute-start | bytes 1290248 | tf_op jit(solution)/shard_map/ppermute | solution.py:29
  32.6 20.2 %collective-permute-start.5 = (bf16[5,336,128]{2,1,0:T(8,128)(2,1)S(1)}, bf16[5,336,128]{2,1,0:T(8,128)(2,1)S(1)}, u32[]{:S(2)}, u32[]{:S(2)}) collective-permute-start(bf16[5,336,128]{2,1,0:T(8,128)(2,1)S(1)} %collective-permute-done.refs_4_.refs_6_), channel_id=1, source_target_pairs={{0,32},{8,40},{16,48},{24,56},{32,64},{40,72},{48,80},{56,88},{64,... | collective-permute-start | bytes 1290248 | tf_op jit(solution)/shard_map/ppermute | solution.py:29
  32.9 14.4 %collective-permute-start.11 = (bf16[5,336,128]{2,1,0:T(8,128)(2,1)}, bf16[5,336,128]{2,1,0:T(8,128)(2,1)}, u32[]{:S(2)}, u32[]{:S(2)}) collective-permute-start(bf16[5,336,128]{2,1,0:T(8,128)(2,1)} %get-tuple-element.39.refs_7_.refs_9_), channel_id=1, source_target_pairs={{0,8},{8,16},{16,24},{24,0},{32,40},{40,48},{48,56},{56,32},{64,72... | collective-permute-start | bytes 1290248 | tf_op jit(solution)/shard_map/ppermute | solution.py:29
  36.2 16.6 %collective-permute-start.9 = (bf16[5,336,128]{2,1,0:T(8,128)(2,1)S(1)}, bf16[5,336,128]{2,1,0:T(8,128)(2,1)S(1)}, u32[]{:S(2)}, u32[]{:S(2)}) collective-permute-start(bf16[5,336,128]{2,1,0:T(8,128)(2,1)S(1)} %collective-permute-done.1.refs_10_.refs_14_), channel_id=1, source_target_pairs={{0,8},{8,16},{16,24},{24,0},{32,40},{40,48},{48,56},{56,32},{64,72... | collective-permute-start | bytes 1290248 | tf_op jit(solution)/shard_map/ppermute | solution.py:29
  42.0 10.9 %collective-permute-start.6 = (bf16[5,336,128]{2,1,0:T(8,128)(2,1)S(1)}, bf16[5,336,128]{2,1,0:T(8,128)(2,1)S(1)}, u32[]{:S(2)}, u32[]{:S(2)}) collective-permute-start(bf16[5,336,128]{2,1,0:T(8,128)(2,1)S(1)} %collective-permute-done.2.refs_3_), channel_id=1, source_target_pairs={{0,96},{8,104},{16,112},{24,120},{32,0},{40,8},{48,16},{56,24},{64... | collective-permute-start | bytes 1290248 | tf_op jit(solution)/shard_map/ppermute | solution.py:29
  42.0 10.9 %collective-permute-start.10 = (bf16[5,336,128]{2,1,0:T(8,128)(2,1)S(1)}, bf16[5,336,128]{2,1,0:T(8,128)(2,1)S(1)}, u32[]{:S(2)}, u32[]{:S(2)}) collective-permute-start(bf16[5,336,128]{2,1,0:T(8,128)(2,1)S(1)} %collective-permute-done.3.refs_9_.refs_11_), channel_id=1, source_target_pairs={{0,24},{8,0},{16,8},{24,16},{32,56},{40,32},{48,40},{56,48},{64,88... | collective-permute-start | bytes 1290248 | tf_op jit(solution)/shard_map/ppermute | solution.py:29
  52.8 0.8 copy-start
  52.9 0.9 copy-start.2
  52.9 1.0 copy-start.1
  52.9 1.2 copy-start.3
  57.6 36.3 %collective-permute-start.12 = (bf16[20,336,128]{2,1,0:T(8,128)(2,1)}, bf16[20,336,128]{2,1,0:T(8,128)(2,1)S(1)}, u32[]{:S(2)}, u32[]{:S(2)}) collective-permute-start(bf16[20,336,128]{2,1,0:T(8,128)(2,1)} %get-tuple-element.44), channel_id=1, source_target_pairs={{0,8},{8,16},{16,24},{24,0},{32,40},{40,48},{48,56},{56,32},{64,72... | collective-permute-start | bytes 5160968 | tf_op jit(solution)/shard_map/ppermute | solution.py:29
  57.7 54.0 %collective-permute-start.13 = (bf16[20,336,128]{2,1,0:T(8,128)(2,1)}, bf16[20,336,128]{2,1,0:T(8,128)(2,1)S(1)}, u32[]{:S(2)}, u32[]{:S(2)}) collective-permute-start(bf16[20,336,128]{2,1,0:T(8,128)(2,1)} %get-tuple-element.45), channel_id=1, source_target_pairs={{0,24},{8,0},{16,8},{24,16},{32,56},{40,32},{48,40},{56,48},{64,88... | collective-permute-start | bytes 5160968 | tf_op jit(solution)/shard_map/ppermute | solution.py:29
  60.9 50.8 %collective-permute-start.14 = (bf16[20,336,128]{2,1,0:T(8,128)(2,1)}, bf16[20,336,128]{2,1,0:T(8,128)(2,1)}, u32[]{:S(2)}, u32[]{:S(2)}) collective-permute-start(bf16[20,336,128]{2,1,0:T(8,128)(2,1)} %get-tuple-element.46), channel_id=1, source_target_pairs={{0,32},{8,40},{16,48},{24,56},{32,64},{40,72},{48,80},{56,88},{64,... | collective-permute-start | bytes 5160968 | tf_op jit(solution)/shard_map/ppermute | solution.py:29
  62.8 48.9 %collective-permute-start.15 = (bf16[20,336,128]{2,1,0:T(8,128)(2,1)}, bf16[20,336,128]{2,1,0:T(8,128)(2,1)}, u32[]{:S(2)}, u32[]{:S(2)}) collective-permute-start(bf16[20,336,128]{2,1,0:T(8,128)(2,1)} %get-tuple-element.47), channel_id=1, source_target_pairs={{0,96},{8,104},{16,112},{24,120},{32,0},{40,8},{48,16},{56,24},{64... | collective-permute-start | bytes 5160968 | tf_op jit(solution)/shard_map/ppermute | solution.py:29
  93.9 17.8 %copy-start.10 = (bf16[20,336,128]{2,1,0:T(8,128)(2,1)}, bf16[20,336,128]{2,1,0:T(8,128)(2,1)S(1)}, u32[]{:S(2)}) copy-start(bf16[20,336,128]{2,1,0:T(8,128)(2,1)S(1)} %collective-permute-done.12.refs_16_) | copy-start | bytes 5160964
  111.7 1.2 copy-start.11
  111.7 26.0 %collective-permute-start.16 = (bf16[20,336,128]{2,1,0:T(8,128)(2,1)}, bf16[20,336,128]{2,1,0:T(8,128)(2,1)S(1)}, u32[]{:S(2)}, u32[]{:S(2)}) collective-permute-start(bf16[20,336,128]{2,1,0:T(8,128)(2,1)} %get-tuple-element.51), channel_id=1, source_target_pairs={{0,16},{8,24},{16,0},{24,8},{32,48},{40,56},{48,32},{56,40},{64,80... | collective-permute-start | bytes 5160968 | tf_op jit(solution)/shard_map/ppermute | solution.py:29
  112.9 25.4 %collective-permute-start.17 = (bf16[20,336,128]{2,1,0:T(8,128)(2,1)}, bf16[20,336,128]{2,1,0:T(8,128)(2,1)S(1)}, u32[]{:S(2)}, u32[]{:S(2)}) collective-permute-start(bf16[20,336,128]{2,1,0:T(8,128)(2,1)} %get-tuple-element.53), channel_id=1, source_target_pairs={{0,64},{8,72},{16,80},{24,88},{32,96},{40,104},{48,112},{56,120},{... | collective-permute-start | bytes 5160968 | tf_op jit(solution)/shard_map/ppermute | solution.py:29
  137.7 1.2 copy-start.8
  138.4 1.2 copy-start.9
Sparse Core Ops, SparseCore 0:
  9.1 103.8 all-gather.1
